TPU v7x, 32 devices: a whole 2x2x4 slice. The times are simulated.
32 devices in a mesh: wa: 16 (over z, y, x), row: 2 (over core).
Axes of the slice: x: 2, y: 2, z: 4, core: 2. Of those that a mesh axis runs over, the one named last changes fastest.
Arguments:
- tokens: bfloat16 [2048, 12288], P('wa', 'row'), may hold values from -6 to 6
- active: int32 [16, 48], replicated, may hold values from 0 to 383, all different within a row; in each aligned block of 16 rows (0 to 15, 16 to 31, ...) at most 2 rows name the same one
- w_up: bfloat16 [12288, 49152], P('row', 'wa'), may hold values from -0.0546875 to 0.0546875
- b_up: float32 [49152], P('wa'), may hold values from -3 to 3
- w_down: bfloat16 [49152, 12288], P('wa', 'row'), may hold values from -0.078125 to 0.078125
- b_down: float32 [12288], P('row'), may hold values from -3 to 3
Outputs:
- mixed: bfloat16 [2048, 12288], P('wa', 'row')
Inputs may be any that keep to these rules, and one draw needn't show every extreme that they name: Row t lists 48 different neuron blocks active for token block t. Every neuron block is named by at least one and at most 2 token blocks, and one by exactly 2.
All inputs are finite; a program needn't handle non-finite values.
Results may differ from a plain program's by a relative error of at most 0.025.
Values may be sent and summed in bfloat16 or wider, within the bound.
No kernel may reach another device: no remote copies, remote signals or barrier semaphores. Data moves between devices by JAX's collectives and lax.ppermute only.
A program may use at most 320 MiB of HBM per device.

v0:
```python
import jax
import jax.numpy as jnp
from jax import lax
from jax.sharding import PartitionSpec as P

BLK = 128
K = 48


def per_device(tokens, active, w_up, b_up, w_down, b_down):
    feat_dev = tokens.shape[1]
    tblocks = active.shape[0]
    owners = lax.axis_size("wa")
    per_owner = w_up.shape[1] // BLK
    nblocks = per_owner * owners
    capacity = max(2, 5 * tblocks * K // (4 * nblocks))
    gathered = lax.all_gather(tokens, "wa", axis=0, tiled=True)
    token_blocks = gathered.reshape(tblocks, BLK, feat_dev)
    owner = lax.axis_index("wa")
    targets = owner * per_owner + jnp.arange(per_owner, dtype=jnp.int32)
    hits = jnp.any(active[:, :, None] == targets[None, None, :], axis=1).astype(jnp.int32)
    running = jnp.cumsum(hits, axis=0)
    slots = jnp.arange(capacity, dtype=jnp.int32) + 1
    picked = hits[:, :, None] * (running[:, :, None] == slots[None, None, :]).astype(jnp.int32)
    block_index = jnp.arange(tblocks, dtype=jnp.int32)
    slot_tok = jnp.sum(picked * block_index[:, None, None], axis=0)
    selected = token_blocks[slot_tok.reshape(-1)].reshape(per_owner, capacity * BLK, feat_dev)
    up_local = w_up.reshape(feat_dev, per_owner, BLK)
    preact = jnp.einsum("jmd,djb->jmb", selected, up_local, preferred_element_type=jnp.float32)
    bias_local = b_up.reshape(per_owner, 1, BLK)
    summed = lax.psum(preact.astype(jnp.bfloat16), "row").astype(jnp.float32)
    hidden = jnp.maximum(summed + bias_local, 0.0).astype(jnp.bfloat16)
    down_local = w_down.reshape(per_owner, BLK, feat_dev)
    contrib = jnp.einsum("jmb,jbd->jmd", hidden, down_local, preferred_element_type=jnp.float32)
    contrib = contrib.reshape(per_owner, capacity, BLK, feat_dev)
    placing = picked.transpose(1, 2, 0).astype(jnp.float32)
    partial_value = jnp.einsum("jct,jcqd->tqd", placing, contrib, precision=lax.Precision.HIGHEST)
    partial_value = partial_value.astype(jnp.bfloat16)
    terms = partial_value.reshape(tblocks * BLK, feat_dev).astype(jnp.float32)
    total = lax.psum_scatter(
        terms.astype(jnp.bfloat16), "wa", scatter_dimension=0, tiled=True
    ).astype(jnp.float32)
    return (total + b_down).astype(jnp.bfloat16)


def solution(mesh):
    in_specs = (P("wa", "row"), P(), P("row", "wa"), P("wa"), P("wa", "row"), P("row"))
    out_specs = P("wa", "row")
    return jax.shard_map(
        per_device, mesh=mesh, in_specs=in_specs, out_specs=out_specs, check_vma=False
    )
```

profile of v0, /device:TPU:0, one launch (start us, length us, event | category | flops | bytes accessed | tf_op | source)
XLA Modules:
  0.0 1027.2 jit_solution(11293157906316432524)
XLA Ops:
  6.5 0.0 all-gather.2.cloned.1.call-start
  6.5 0.7 all-gather.2.cloned.1.call-update
  7.3 0.0 all-reduce.2.cloned.1.call-start
  7.3 1.1 compare_reduce_fusion
  8.5 0.1 multiply_reduce_fusion
  8.6 0.1 copy.10
  8.7 0.1 reshape.70
  8.8 275.3 %all-gather.2.cloned.1.call-done = bf16[2048,6144]{1,0:T(8,128)(2,1)} async-done(((bf16[128,6144]{1,0:T(8,128)(2,1)}), bf16[2048,6144]{1,0:T(8,128)(2,1)}) %all-gather.2.cloned.1.call-update) | async-done | bytes 25165840 | tf_op jit(solution)/shard_map/all_gather | solution.py:17
  284.1 33.4 %gather_fusion = bf16[48,128,6144]{2,1,0:T(8,128)(2,1)} fusion(bf16[16,128,6144]{2,1,0:T(8,128)(2,1)} %bitcast.32, s32[1024]{0:T(1024)S(1)} %pad_clamp_fusion), kind=kCustom, calls=%fused_computation | custom fusion | bytes 150995136 | tf_op jit(solution)/shard_map/gather | solution.py:27
  317.5 0.0 copy-start
  317.5 38.4 %fusion.7 = bf16[24,256,128]{2,1,0:T(8,128)(2,1)} fusion(bf16[24,256,6144]{2,1,0:T(8,128)(2,1)} %bitcast.5, bf16[6144,3072]{1,0:T(8,128)(2,1)} %param.8), kind=kOutput, calls=%fused_computation.9 | convolution fusion | flops 9664462848 | bytes 114819072 | tf_op jit(solution)/shard_map/jmd,djb->jmb/dot_general | solution.py:29
  355.9 0.0 all-reduce.2.cloned.1.call-update
  355.9 0.0 reduce-scatter.2.cloned.1.call-start
  356.0 18.7 %all-reduce.2.cloned.1.call-done = bf16[24,256,128]{2,1,0:T(8,128)(2,1)} async-done(((bf16[24,256,128]{2,1,0:T(8,128)(2,1)}), bf16[24,256,128]{2,1,0:T(8,128)(2,1)}) %all-reduce.2.cloned.1.call-update) | async-done | bytes 1572880 | tf_op jit(solution)/shard_map/psum | solution.py:31
  374.7 0.0 copy-done
  374.7 64.3 %fusion.10 = f32[24,256,6144]{2,1,0:T(8,128)} fusion(bf16[24,128,6144]{2,1,0:T(8,128)(2,1)} %bitcast.34, bf16[24,256,128]{2,1,0:T(8,128)(2,1)} %all-reduce.2.cloned.1.call-done, f32[24,128]{1,0:T(8,128)S(1)} %bitcast.35), kind=kOutput, calls=%fused_computation.10 | convolution fusion | flops 9666822144 | bytes 190328832 | tf_op jit(solution)/shard_map/jmb,jbd->jmd/dot_general | solution.py:34
  439.0 189.0 %bitcast_convert_fusion = bf16[16,128,6144]{2,0,1:T(8,128)(2,1)} fusion(f32[24,2,128,6144]{3,2,1,0:T(8,128)} %bitcast.8, s32[24,16]{0,1:T(8,128)S(1)} %get-tuple-element.5, s32[24,16]{0,1:T(8,128)S(1)} %bitcast.36, s32[2]{0:T(128)S(1)} %iota_add_fusion), kind=kOutput, calls=%fused_computation.3 | convolution fusion | flops 7260342272 | bytes 176163840 | tf_op jit(solution)/shard_map/jct,jcqd->tqd/dot_general | solution.py:37
  628.0 26.8 %copy.13 = bf16[16,128,6144]{2,1,0:T(8,128)(2,1)} copy(bf16[16,128,6144]{2,0,1:T(8,128)(2,1)} %bitcast_convert_fusion) | data formatting | bytes 50331648 | tf_op jit(solution)/shard_map/convert_element_type | solution.py:38
  654.8 0.0 copy-start.1
  654.8 0.0 reduce-scatter.2.cloned.1.call-update
  654.8 362.9 %reduce-scatter.2.cloned.1.call-done = bf16[128,6144]{1,0:T(8,128)(2,1)} async-done(((bf16[2048,6144]{1,0:T(8,128)(2,1)}), bf16[128,6144]{1,0:T(8,128)(2,1)}) %reduce-scatter.2.cloned.1.call-update) | async-done | bytes 1572880 | tf_op jit(solution)/shard_map/reduce_scatter | solution.py:40
  1017.8 0.0 copy-done.1
  1017.8 2.9 add_convert_fusion
  (6 shorter events, 0.1 us)
Async XLA Ops:
  6.5 277.6 %all-gather.2.cloned.1.call-start = ((), (), s32[]{:S(2)}) async-start(), calls=%async_computation.1 | async-start | bytes 26738688 | tf_op jit(solution)/shard_map/all_gather | solution.py:17
  7.3 367.4 %all-reduce.2.cloned.1.call-start = ((), (), s32[]{:S(2)}) async-start(), calls=%async_computation.2 | async-start | bytes 3145728 | tf_op jit(solution)/shard_map/psum | solution.py:31
  317.5 57.2 %copy-start = (f32[3072]{0:T(1024)S(1)}, f32[3072]{0:T(1024)}, u32[]{:S(2)}) copy-start(f32[3072]{0:T(1024)} %param.9) | copy-start | bytes 36868
  355.9 661.8 %reduce-scatter.2.cloned.1.call-start = ((), (), s32[]{:S(2)}) async-start(), calls=%async_computation.3 | async-start | bytes 26738688 | tf_op jit(solution)/shard_map/reduce_scatter | solution.py:40
  654.8 363.0 %copy-start.1 = (f32[6144]{0:T(1024)S(1)}, f32[6144]{0:T(1024)}, u32[]{:S(2)}) copy-start(f32[6144]{0:T(1024)} %param.11) | copy-start | bytes 73732
Sparse Core Ops, SparseCore 0:
  10.1 273.9 all-gather.1
  356.1 18.5 all-reduce.1
  654.9 362.7 reduce-scatter.1
where the time goes:
time: 1030 us
  waiting for transfers between devices  658 us (64%)
  matrix products  292 us (28%)
  local copies, waits for them, and re-layouts  60.4 us (6%)
  between operations  13.2 us (1%)
    reduce_scatter x1, waiting for transfers between devices, per_device(): lax.psum_scatter(terms.astype(jnp.bfloat16), 'wa', scatter_dimension=0, t...  363 us
    all_gather x1, waiting for transfers between devices, per_device(): gathered = lax.all_gather(tokens, 'wa', axis=0, tiled=True)  275 us
    dot_general x1, matrix products, per_device(): jnp.einsum('jct,jcqd->tqd', placing, contrib, precision=lax.Precision.HIG...  189 us
    dot_general x1, matrix products, per_device(): jnp.einsum('jmb,jbd->jmd', hidden, down_local, preferred_element_type=jnp...  64.3 us
    dot_general x1, matrix products, per_device(): jnp.einsum('jmd,djb->jmb', selected, up_local, preferred_element_type=jnp...  38.4 us
    gather x1, local copies, waits for them, and re-layouts, per_device(): token_blocks[slot_tok.reshape(-1)]  33.4 us
    convert_element_type x1, local copies, waits for them, and re-layouts, per_device(): partial_value = partial_value.astype(jnp.bfloat16)  26.8 us
  transfers between devices with their start and end apart: 3, of which 3 were waited for; matrix products, arithmetic and copies ran while one was open for 0% of the time, Pallas kernels for 0%

commit v1 on v0

--- a/solution.py
+++ b/solution.py
@@ -1,13 +1,261 @@
+import functools
+
 import jax
 import jax.numpy as jnp
 from jax import lax
+from jax.experimental import pallas as pl
+from jax.experimental.pallas import tpu as pltpu
 from jax.sharding import PartitionSpec as P
 
 BLK = 128
 K = 48
-
-
-def per_device(tokens, active, w_up, b_up, w_down, b_down):
+HALF = BLK // 2
+PLANE = 4
+LAYERS = 4
+DEPTH = 3
+VMEM_BYTES = 56 * 1024 * 1024
+
+
+def stream(meta, per_owner, fetch, use):
+    count = meta[0]
+
+    def block(step):
+        return lax.rem(meta[1 + step], per_owner)
+
+    for ahead in range(DEPTH - 1):
+        @pl.when(ahead < count)
+        def _():
+            fetch(block(ahead), ahead).start()
+
+    def body(step, carry):
+        nearest = step + DEPTH - 1
+
+        @pl.when(nearest < count)
+        def _():
+            fetch(block(nearest), lax.rem(nearest, DEPTH)).start()
+
+        slot = lax.rem(step, DEPTH)
+        fetch(block(step), slot).wait()
+        use(step, slot)
+        return carry
+
+    lax.fori_loop(0, count, body, 0)
+
+
+def up_kernel(per_owner, meta, *refs):
+    parts, (w_ref, own_ref, send_ref, rows, held, row_sems, sems) = refs[:2 * PLANE], refs[2 * PLANE:]
+    copies = []
+    for at, part in enumerate(parts):
+        place = rows.at[at // 2, pl.ds((at % 2) * HALF, HALF)]
+        copies.append(pltpu.make_async_copy(part, place, row_sems.at[at]))
+    for copy in copies:
+        copy.start()
+
+    def fetch(block, slot):
+        cols = pl.ds(pl.multiple_of(block * BLK, BLK), BLK)
+        return pltpu.make_async_copy(w_ref.at[:, cols], held.at[slot], sems.at[slot])
+
+    for copy in copies:
+        copy.wait()
+
+    def use(step, slot):
+        offset = lax.div(meta[1 + step], per_owner)
+        preact = jnp.dot(rows[offset], held[slot], preferred_element_type=jnp.float32)
+        own_ref[step] = preact
+        send_ref[step] = preact.astype(jnp.bfloat16)
+
+    stream(meta, per_owner, fetch, use)
+
+
+def estimate(feat):
+    return pl.CostEstimate(flops=2 * 24 * BLK * BLK * feat, bytes_accessed=24 * BLK * feat * 2, transcendentals=0)
+
+
+def up_group(meta, parts, w_up, slots):
+    feat = w_up.shape[0]
+    per_owner = w_up.shape[1] // BLK
+    return pl.pallas_call(
+        functools.partial(up_kernel, per_owner),
+        in_specs=[pl.BlockSpec(memory_space=pltpu.SMEM)] + [pl.BlockSpec(memory_space=pl.ANY)] * (len(parts) + 1),
+        out_specs=[pl.BlockSpec(memory_space=pltpu.VMEM)] * 2,
+        scratch_shapes=[
+            pltpu.VMEM((PLANE, BLK, feat), jnp.bfloat16),
+            pltpu.VMEM((DEPTH, feat, BLK), jnp.bfloat16),
+            pltpu.SemaphoreType.DMA((len(parts),)),
+            pltpu.SemaphoreType.DMA((DEPTH,)),
+        ],
+        out_shape=[
+            jax.ShapeDtypeStruct((slots, BLK, BLK), jnp.float32),
+            jax.ShapeDtypeStruct((slots, BLK, BLK), jnp.bfloat16),
+        ],
+        compiler_params=pltpu.CompilerParams(vmem_limit_bytes=VMEM_BYTES),
+        cost_estimate=estimate(feat),
+        name="up_group",
+    )(meta, *parts, w_up)
+
+
+def down_kernel(per_owner, meta, own_ref, other_ref, bias_ref, w_ref, *refs):
+    outs, (total, held, sems) = refs[:2 * PLANE], refs[2 * PLANE:]
+    count = meta[0]
+    width = total.shape[1]
+    piece = width // 6 if width % (6 * BLK) == 0 else width
+    for out in outs:
+        out[...] = jnp.zeros_like(out)
+
+    def fetch(block, slot):
+        rows = pl.ds(pl.multiple_of(block * BLK, BLK), BLK)
+        return pltpu.make_async_copy(w_ref.at[rows], held.at[slot], sems.at[slot])
+
+    def use(step, slot):
+        offset = lax.div(meta[1 + step], per_owner)
+        block = lax.rem(meta[1 + step], per_owner)
+        before = lax.div(meta[jnp.maximum(step, 1)], per_owner)
+        after = lax.div(meta[2 + step], per_owner)
+        first = (step == 0) | (before != offset)
+        last = (step >= count - 1) | (after != offset)
+        preact = own_ref[step] + other_ref[step].astype(jnp.float32) + bias_ref[block]
+        hidden = jnp.maximum(preact, 0.0).astype(jnp.bfloat16)
+        for at in range(0, width, piece):
+            cols = pl.ds(at, piece)
+            term = jnp.dot(hidden, held[slot, :, cols], preferred_element_type=jnp.float32)
+            total[:, cols] = jnp.where(first, 0.0, total[:, cols]) + term
+
+        for o in range(PLANE):
+            @pl.when(last & (offset == o))
+            def _():
+                outs[2 * o][...] = total[:HALF].astype(jnp.bfloat16)
+                outs[2 * o + 1][...] = total[HALF:].astype(jnp.bfloat16)
+
+    stream(meta, per_owner, fetch, use)
+
+
+def down_group(meta, own, other, bias, w_down):
+    feat = w_down.shape[1]
+    per_owner = w_down.shape[0] // BLK
+    whole = pl.BlockSpec(memory_space=pltpu.VMEM)
+    outs = pl.pallas_call(
+        functools.partial(down_kernel, per_owner),
+        in_specs=[pl.BlockSpec(memory_space=pltpu.SMEM), whole, whole, whole, pl.BlockSpec(memory_space=pl.ANY)],
+        out_specs=[whole] * (2 * PLANE),
+        scratch_shapes=[
+            pltpu.VMEM((BLK, feat), jnp.float32),
+            pltpu.VMEM((DEPTH, BLK, feat), jnp.bfloat16),
+            pltpu.SemaphoreType.DMA((DEPTH,)),
+        ],
+        out_shape=[jax.ShapeDtypeStruct((HALF, feat), jnp.bfloat16)] * (2 * PLANE),
+        compiler_params=pltpu.CompilerParams(vmem_limit_bytes=VMEM_BYTES),
+        cost_estimate=estimate(feat),
+        name="down_group",
+    )(meta, own, other, bias, w_down)
+    return [(outs[2 * o], outs[2 * o + 1]) for o in range(PLANE)]
+
+
+def in_plane(value, bit):
+    owners = LAYERS * PLANE
+    return lax.ppermute(value, "wa", [(w, w ^ bit) for w in range(owners)])
+
+
+def along_z(value, *hops):
+    pairs = [(a * PLANE + q, b * PLANE + q) for a, b in hops for q in range(PLANE)]
+    return lax.ppermute(value, "wa", pairs)
+
+
+def gather_plane(block):
+    a0, b0 = block
+    a1, b2 = in_plane(a0, 1), in_plane(b0, 2)
+    a2, a3 = in_plane(a0, 2), in_plane(a1, 2)
+    b1, b3 = in_plane(b0, 1), in_plane(b2, 1)
+    return [a0, b0, a1, b1, a2, b2, a3, b3]
+
+
+def add(*terms):
+    total = terms[0].astype(jnp.float32)
+    for term in terms[1:]:
+        total = total + term.astype(jnp.float32)
+    return total
+
+
+def narrow(*terms):
+    return add(*terms).astype(jnp.bfloat16)
+
+
+def reduce_plane(partial):
+    (a0, b0), (a1, b1), (a2, b2), (a3, b3) = partial
+    from_a2, from_a3 = in_plane(a2, 2), in_plane(a3, 2)
+    from_b1, from_b3 = in_plane(b1, 1), in_plane(b3, 1)
+    from_a1 = in_plane(narrow(a1, from_a3), 1)
+    from_b2 = in_plane(narrow(b2, from_b3), 2)
+    return add(a0, from_a2, from_a1), add(b0, from_b1, from_b2)
+
+
+def join(halves):
+    return jnp.concatenate(halves, axis=0)
+
+
+def pair_lists(active, owner, per_owner):
+    layer, cell = owner // PLANE, owner % PLANE
+    order = jnp.array([[0, 1, 2, 3], [1, 2, 3, 0], [2, 1, 0, 3], [3, 2, 1, 0]], jnp.int32)
+    layers = jnp.sum(jnp.where(jnp.arange(LAYERS)[:, None] == layer, order, 0), axis=0)
+    blocks = layers[:, None] * PLANE + (cell ^ jnp.arange(PLANE, dtype=jnp.int32))[None, :]
+    targets = owner * per_owner + jnp.arange(per_owner, dtype=jnp.int32)
+    hits = jnp.any(active[:, :, None] == targets[None, None, :], axis=1)
+    is_block = blocks[:, :, None] == jnp.arange(active.shape[0], dtype=jnp.int32)
+    hits = jnp.any(is_block[..., None] & hits[None, None], axis=2)
+    hits = hits.reshape(LAYERS, PLANE * per_owner).astype(jnp.int32)
+    slots = 2 * per_owner
+    number = jnp.cumsum(hits, axis=1) * hits
+    codes = jnp.arange(PLANE * per_owner, dtype=jnp.int32)
+    wanted = jnp.arange(slots + 8, dtype=jnp.int32) + 1
+    lists = jnp.sum(jnp.where(number[:, :, None] == wanted, codes[None, :, None], 0), axis=1)
+    counts = jnp.sum(hits, axis=1, keepdims=True)
+    return jnp.concatenate([counts, lists], axis=1), slots
+
+
+def by_layers(tokens, active, w_up, b_up, w_down, b_down):
+    per_owner = w_up.shape[1] // BLK
+    owner = lax.axis_index("wa")
+    layer = owner // PLANE
+    inner = (layer == 1) | (layer == 2)
+    meta, slots = pair_lists(active, owner, per_owner)
+    bias = b_up.reshape(per_owner, 1, BLK)
+
+    inward = along_z(tokens, (0, 1), (3, 2))
+    across = along_z(tokens, (1, 2), (2, 1))
+    outward = along_z(tokens, (1, 0), (2, 3))
+    across2 = along_z(inward, (1, 2), (2, 1))
+    outward2 = along_z(across, (1, 0), (2, 3))
+    outward3 = along_z(across2, (1, 0), (2, 3))
+
+    def halves(inside, outside):
+        return [jnp.where(inner, inside[rows], outside[rows]) for rows in (slice(0, HALF), slice(HALF, BLK))]
+
+    groups = [
+        [tokens[:HALF], tokens[HALF:]],
+        halves(across, outward),
+        halves(across2, outward2),
+        halves(inward, outward3),
+    ]
+    partial = []
+    for at, group in enumerate(groups):
+        parts = gather_plane(group)
+        own, send = up_group(meta[at], parts, w_up, slots)
+        other = lax.ppermute(send, "row", [(0, 1), (1, 0)])
+        partial.append(down_group(meta[at], own, other, bias, w_down))
+
+    sums = {at: join(reduce_plane(partial[at])) for at in (2, 3, 1, 0)}
+    from_corner = along_z(sums[3].astype(jnp.bfloat16), (0, 1), (3, 2))
+    second = narrow(sums[2], from_corner)
+    third = narrow(sums[3], along_z(second, (1, 2), (2, 1)))
+    first = narrow(sums[1], along_z(second, (0, 1), (3, 2)))
+    last = [
+        along_z(third, (1, 0), (2, 3)),
+        along_z(first, (1, 2), (2, 1)),
+        along_z(first, (0, 1), (3, 2)),
+    ]
+    return (add(sums[0], *last) + b_down).astype(jnp.bfloat16)
+
+
+def general(tokens, active, w_up, b_up, w_down, b_down):
     feat_dev = tokens.shape[1]
     tblocks = active.shape[0]
     owners = lax.axis_size("wa")
@@ -35,15 +283,14 @@
     contrib = contrib.reshape(per_owner, capacity, BLK, feat_dev)
     placing = picked.transpose(1, 2, 0).astype(jnp.float32)
     partial_value = jnp.einsum("jct,jcqd->tqd", placing, contrib, precision=lax.Precision.HIGHEST)
-    partial_value = partial_value.astype(jnp.bfloat16)
-    terms = partial_value.reshape(tblocks * BLK, feat_dev).astype(jnp.float32)
-    total = lax.psum_scatter(
-        terms.astype(jnp.bfloat16), "wa", scatter_dimension=0, tiled=True
-    ).astype(jnp.float32)
+    terms = partial_value.reshape(tblocks * BLK, feat_dev).astype(jnp.bfloat16)
+    total = lax.psum_scatter(terms, "wa", scatter_dimension=0, tiled=True).astype(jnp.float32)
     return (total + b_down).astype(jnp.bfloat16)
 
 
 def solution(mesh):
+    sizes = (mesh.shape["wa"], mesh.shape["row"])
+    per_device = by_layers if sizes == (LAYERS * PLANE, 2) else general
     in_specs = (P("wa", "row"), P(), P("row", "wa"), P("wa"), P("wa", "row"), P("row"))
     out_specs = P("wa", "row")
     return jax.shard_map(

time: 1030 us -> 577 us (0.56)
  waiting for transfers between devices: 658 us -> 323 us
  matrix products: 292 us -> 0 us
  Pallas kernels: 0 us -> 123 us
  starting transfers between devices: 0.08 us -> 105 us
  local copies, waits for them, and re-layouts: 60.4 us -> 8.81 us
  between operations: 13.2 us -> 0.86 us
  other arithmetic: 4.12 us -> 15.3 us
    reduce_scatter x1 -> x0, waiting for transfers between devices: 363 us -> none  [per_device(): lax.psum_scatter(terms.astype(jnp.bfloat16), 'wa', scatter_dimension=0, t...]
    ppermute x0 -> x64, waiting for transfers between devices: none -> 323 us  [the longest x48 239 us: in_plane(): return lax.ppermute(value, 'wa', [(w, w ^ bit) for w in range(owners)])]
    dot_general x3 -> x0, matrix products: 292 us -> none  [the longest x1 189 us: per_device(): jnp.einsum('jct,jcqd->tqd', placing, contrib, precision=lax.Precision.HIG...]
    all_gather x1 -> x0, waiting for transfers between devices: 275 us -> none  [per_device(): gathered = lax.all_gather(tokens, 'wa', axis=0, tiled=True)]
    pallas_call x0 -> x8, Pallas kernels: none -> 123 us  [the longest x4 61.8 us: down_group(): pl.pallas_call(functools.partial(down_kernel, per_owner), in_specs=[pl.Bl...]
    ppermute x0 -> x64, starting transfers between devices: none -> 105 us  [the longest x48 61.1 us: in_plane(): return lax.ppermute(value, 'wa', [(w, w ^ bit) for w in range(owners)])]
    gather x1 -> x0, local copies, waits for them, and re-layouts: 33.4 us -> none  [per_device(): token_blocks[slot_tok.reshape(-1)]]
    convert_element_type x1 -> x0, local copies, waits for them, and re-layouts: 26.8 us -> none  [per_device(): partial_value = partial_value.astype(jnp.bfloat16)]
  transfers between devices with their start and end apart: 3 -> 64, of which waited for: 3 -> 24; matrix products, arithmetic and copies ran while one was open for 0% -> 3% of each run, Pallas kernels for 0% -> 21%
where the time goes in v1:
time: 577 us; the launch traced here: 576 us
  waiting for transfers between devices  323 us (56%)
  Pallas kernels  123 us (21%)
  starting transfers between devices  105 us (18%)
  other arithmetic  15.3 us (3%)
  local copies, waits for them, and re-layouts  8.81 us (2%)
    ppermute x48, waiting for transfers between devices, in_plane(): return lax.ppermute(value, 'wa', [(w, w ^ bit) for w in range(owners)])  239 us
    ppermute x12, waiting for transfers between devices, along_z(): return lax.ppermute(value, 'wa', pairs)  84.6 us
    pallas_call x4, Pallas kernels, down_group(): pl.pallas_call(functools.partial(down_kernel, per_owner), in_specs=[pl.Bl...  61.8 us
    pallas_call x4, Pallas kernels, up_group(): pl.pallas_call(functools.partial(up_kernel, per_owner), in_specs=[pl.Bloc...  61.6 us
    ppermute x48, starting transfers between devices, in_plane(): return lax.ppermute(value, 'wa', [(w, w ^ bit) for w in range(owners)])  61.1 us
    ppermute x12, starting transfers between devices, along_z(): return lax.ppermute(value, 'wa', pairs)  43.5 us
  transfers between devices with their start and end apart: 64, of which 24 were waited for; matrix products, arithmetic and copies ran while one was open for 3% of the time, Pallas kernels for 21%

profile of v1, /device:TPU:0, one launch (start us, length us, event | category | flops | bytes accessed | tf_op | source)
XLA Modules:
  0.0 576.4 jit_solution(14417633881744075605)
XLA Ops:
  11.0 32.9 %collective-permute-done.refs_2_ = bf16[64,6144]{1,0:T(8,128)(2,1)} collective-permute-done((bf16[64,6144]{1,0:T(8,128)(2,1)S(1)}, bf16[64,6144]{1,0:T(8,128)(2,1)}, u32[]{:S(2)}, u32[]{:S(2)}) %collective-permute-start) | collective-permute-done | bytes 786464 | tf_op jit(solution)/shard_map/ppermute | solution.py:155
  51.2 15.1 %collective-permute-done.4.refs_6_ = bf16[64,6144]{1,0:T(8,128)(2,1)S(1)} collective-permute-done((bf16[64,6144]{1,0:T(8,128)(2,1)}, bf16[64,6144]{1,0:T(8,128)(2,1)S(1)}, u32[]{:S(2)}, u32[]{:S(2)}) %collective-permute-start.4) | collective-permute-done | bytes 786464 | tf_op jit(solution)/shard_map/ppermute | solution.py:155
  67.4 15.3 %up_group.4 = (f32[48,128,128]{2,1,0:T(8,128)}, bf16[48,128,128]{2,1,0:T(8,128)(2,1)}) custom-call(s32[57]{0:T(128)} %get-tuple-element.96.meta, bf16[64,6144]{1,0:T(8,128)(2,1)} %copy-done.7, bf16[64,6144]{1,0:T(8,128)(2,1)} %copy-done.6, bf16[64,6144]{1,0:T(8,128)(2,1)} %collective-permute-done.refs_2_, bf16[64,6144]{1,0:T(8,128)(2,1)} %collective-permute-done.1.refs_3_, ...), custom_call_target="tpu_custom_call" | custom-call | flops 4831838208 | bytes 37748736 | tf_op jit(solution)/shard_map/up_group/pallas_call | solution.py:77
  91.2 15.3 %down_group.4 = (bf16[64,6144]{1,0:T(8,128)(2,1)}, bf16[64,6144]{1,0:T(8,128)(2,1)}, bf16[64,6144]{1,0:T(8,128)(2,1)}, bf16[64,6144]{1,0:T(8,128)(2,1)}, bf16[64...) custom-call(s32[57]{0:T(128)} %get-tuple-element.96.meta, ...), custom_call_target="tpu_custom_call" | custom-call | flops 4831838208 | bytes 37748736 | tf_op jit(solution)/shard_map/down_group/pallas_call | solution.py:136
  111.0 15.1 %collective-permute-done.30 = bf16[128,6144]{1,0:T(8,128)(2,1)S(1)} collective-permute-done((bf16[128,6144]{1,0:T(8,128)(2,1)}, bf16[128,6144]{1,0:T(8,128)(2,1)S(1)}, u32[]{:S(2)}, u32[]{:S(2)}) %collective-permute-start.30) | collective-permute-done | bytes 1572896 | tf_op jit(solution)/shard_map/ppermute | solution.py:160
  129.9 14.9 %collective-permute-done.52.refs_6_ = bf16[64,6144]{1,0:T(8,128)(2,1)S(1)} collective-permute-done((bf16[64,6144]{1,0:T(8,128)(2,1)}, bf16[64,6144]{1,0:T(8,128)(2,1)S(1)}, u32[]{:S(2)}, u32[]{:S(2)}) %collective-permute-start.52) | collective-permute-done | bytes 786464 | tf_op jit(solution)/shard_map/ppermute | solution.py:155
  147.7 15.3 %up_group.7 = (f32[48,128,128]{2,1,0:T(8,128)}, bf16[48,128,128]{2,1,0:T(8,128)(2,1)}) custom-call(s32[57]{0:T(128)} %get-tuple-element.94.meta, bf16[64,6144]{1,0:T(8,128)(2,1)} %copy-done.5, bf16[64,6144]{1,0:T(8,128)(2,1)} %copy-done.4, bf16[64,6144]{1,0:T(8,128)(2,1)} %collective-permute-done.48.refs_2_, ...), custom_call_target="tpu_custom_call" | custom-call | flops 4831838208 | bytes 37748736 | tf_op jit(solution)/shard_map/up_group/pallas_call | solution.py:77
  187.4 15.6 %down_group.7 = (bf16[64,6144]{1,0:T(8,128)(2,1)}, bf16[64,6144]{1,0:T(8,128)(2,1)}, bf16[64,6144]{1,0:T(8,128)(2,1)}, bf16[64,6144]{1,0:T(8,128)(2,1)}, bf16[64...) custom-call(s32[57]{0:T(128)} %get-tuple-element.94.meta, ...), custom_call_target="tpu_custom_call" | custom-call | flops 4831838208 | bytes 37748736 | tf_op jit(solution)/shard_map/down_group/pallas_call | solution.py:136
  222.7 15.5 %up_group.6 = (f32[48,128,128]{2,1,0:T(8,128)}, bf16[48,128,128]{2,1,0:T(8,128)(2,1)}) custom-call(s32[57]{0:T(128)} %get-tuple-element.95.meta, bf16[64,6144]{1,0:T(8,128)(2,1)} %copy-done.1, bf16[64,6144]{1,0:T(8,128)(2,1)} %copy-done, bf16[64,6144]{1,0:T(8,128)(2,1)} %collective-permute-done.31.refs_2_, bf16[64,6144]{1,0:T(8,128)(2,1)} %collective-permute-done.32.refs_3_, ...), custom_call_target="tpu_custom_call" | custom-call | flops 4831838208 | bytes 37748736 | tf_op jit(solution)/shard_map/up_group/pallas_call | solution.py:77
  252.0 10.5 %collective-permute-done.18.refs_4_ = bf16[64,6144]{1,0:T(8,128)(2,1)} collective-permute-done((bf16[64,6144]{1,0:T(8,128)(2,1)S(1)}, bf16[64,6144]{1,0:T(8,128)(2,1)}, u32[]{:S(2)}, u32[]{:S(2)}) %collective-permute-start.18) | collective-permute-done | bytes 786464 | tf_op jit(solution)/shard_map/ppermute | solution.py:155
  264.0 15.3 %collective-permute-done.20.refs_6_ = bf16[64,6144]{1,0:T(8,128)(2,1)S(1)} collective-permute-done((bf16[64,6144]{1,0:T(8,128)(2,1)}, bf16[64,6144]{1,0:T(8,128)(2,1)S(1)}, u32[]{:S(2)}, u32[]{:S(2)}) %collective-permute-start.20) | collective-permute-done | bytes 786464 | tf_op jit(solution)/shard_map/ppermute | solution.py:155
  281.7 15.5 %up_group.5 = (f32[48,128,128]{2,1,0:T(8,128)}, bf16[48,128,128]{2,1,0:T(8,128)(2,1)}) custom-call(s32[57]{0:T(128)} %get-tuple-element.93.meta, bf16[64,6144]{1,0:T(8,128)(2,1)} %copy-done.3, bf16[64,6144]{1,0:T(8,128)(2,1)} %copy-done.2, bf16[64,6144]{1,0:T(8,128)(2,1)} %collective-permute-done.16.refs_2_, bf16[64,6144]{1,0:T(8,128)(2,1)} %copy-done.28, ...), custom_call_target="tpu_custom_call" | custom-call | flops 4831838208 | bytes 37748736 | tf_op jit(solution)/shard_map/up_group/pallas_call | solution.py:77
  298.4 15.5 %down_group.6 = (bf16[64,6144]{1,0:T(8,128)(2,1)}, bf16[64,6144]{1,0:T(8,128)(2,1)}, bf16[64,6144]{1,0:T(8,128)(2,1)}, bf16[64,6144]{1,0:T(8,128)(2,1)}, bf16[64...) custom-call(s32[57]{0:T(128)} %get-tuple-element.95.meta, ...), custom_call_target="tpu_custom_call" | custom-call | flops 4831838208 | bytes 37748736 | tf_op jit(solution)/shard_map/down_group/pallas_call | solution.py:136
  316.2 18.3 %collective-permute-done.39 = bf16[64,6144]{1,0:T(8,128)(2,1)S(1)} collective-permute-done((bf16[64,6144]{1,0:T(8,128)(2,1)}, bf16[64,6144]{1,0:T(8,128)(2,1)S(1)}, u32[]{:S(2)}, u32[]{:S(2)}) %collective-permute-start.39) | collective-permute-done | bytes 786464 | tf_op jit(solution)/shard_map/ppermute | solution.py:155
  336.3 15.4 %down_group.5 = (bf16[64,6144]{1,0:T(8,128)(2,1)}, bf16[64,6144]{1,0:T(8,128)(2,1)}, bf16[64,6144]{1,0:T(8,128)(2,1)}, bf16[64,6144]{1,0:T(8,128)(2,1)}, bf16[64...) custom-call(s32[57]{0:T(128)} %get-tuple-element.93.meta, ...), custom_call_target="tpu_custom_call" | custom-call | flops 4831838208 | bytes 37748736 | tf_op jit(solution)/shard_map/down_group/pallas_call | solution.py:136
  355.2 17.4 %collective-permute-done.24 = bf16[64,6144]{1,0:T(8,128)(2,1)S(1)} collective-permute-done((bf16[64,6144]{1,0:T(8,128)(2,1)}, bf16[64,6144]{1,0:T(8,128)(2,1)S(1)}, u32[]{:S(2)}, u32[]{:S(2)}) %collective-permute-start.24) | collective-permute-done | bytes 786464 | tf_op jit(solution)/shard_map/ppermute | solution.py:155
  374.3 16.0 %collective-permute-done.27 = bf16[64,6144]{1,0:T(8,128)(2,1)S(1)} collective-permute-done((bf16[64,6144]{1,0:T(8,128)(2,1)S(1)}, bf16[64,6144]{1,0:T(8,128)(2,1)S(1)}, u32[]{:S(2)}, u32[]{:S(2)}) %collective-permute-start.27) | collective-permute-done | bytes 786464 | tf_op jit(solution)/shard_map/ppermute | solution.py:155
  392.6 18.2 %collective-permute-done.25 = bf16[64,6144]{1,0:T(8,128)(2,1)S(1)} collective-permute-done((bf16[64,6144]{1,0:T(8,128)(2,1)S(1)}, bf16[64,6144]{1,0:T(8,128)(2,1)S(1)}, u32[]{:S(2)}, u32[]{:S(2)}) %collective-permute-start.25) | collective-permute-done | bytes 786464 | tf_op jit(solution)/shard_map/ppermute | solution.py:155
  412.5 12.3 %collective-permute-done.26 = bf16[64,6144]{1,0:T(8,128)(2,1)S(1)} collective-permute-done((bf16[64,6144]{1,0:T(8,128)(2,1)S(1)}, bf16[64,6144]{1,0:T(8,128)(2,1)S(1)}, u32[]{:S(2)}, u32[]{:S(2)}) %collective-permute-start.26) | collective-permute-done | bytes 786464 | tf_op jit(solution)/shard_map/ppermute | solution.py:155
  428.9 26.6 %collective-permute-done.40 = bf16[64,6144]{1,0:T(8,128)(2,1)S(1)} collective-permute-done((bf16[64,6144]{1,0:T(8,128)(2,1)S(1)}, bf16[64,6144]{1,0:T(8,128)(2,1)S(1)}, u32[]{:S(2)}, u32[]{:S(2)}) %collective-permute-start.40) | collective-permute-done | bytes 786464 | tf_op jit(solution)/shard_map/ppermute | solution.py:155
  469.1 21.7 %collective-permute-done.44 = bf16[128,6144]{1,0:T(8,128)(2,1)S(1)} collective-permute-done((bf16[128,6144]{1,0:T(8,128)(2,1)S(1)}, bf16[128,6144]{1,0:T(8,128)(2,1)S(1)}, u32[]{:S(2)}, u32[]{:S(2)}) %collective-permute-start.44) | collective-permute-done | bytes 1572896 | tf_op jit(solution)/shard_map/ppermute | solution.py:160
  514.5 20.5 %collective-permute-done.61 = bf16[128,6144]{1,0:T(8,128)(2,1)S(1)} collective-permute-done((bf16[128,6144]{1,0:T(8,128)(2,1)S(1)}, bf16[128,6144]{1,0:T(8,128)(2,1)S(1)}, u32[]{:S(2)}, u32[]{:S(2)}) %collective-permute-start.61) | collective-permute-done | bytes 1572896 | tf_op jit(solution)/shard_map/ppermute | solution.py:160
  538.5 13.5 %collective-permute-start.63 = (bf16[128,6144]{1,0:T(8,128)(2,1)S(1)}, bf16[128,6144]{1,0:T(8,128)(2,1)S(1)}, u32[]{:S(2)}, u32[]{:S(2)}) collective-permute-start(bf16[128,6144]{1,0:T(8,128)(2,1)S(1)} %fusion.5), channel_id=1, source_target_pairs={{0,8},{2,10},{4,12},{6,14},{24,16},{26,18},{28,20},{30,22},{1,9},{... | collective-permute-start | bytes 4718600 | tf_op jit(solution)/shard_map/ppermute | solution.py:160
  554.8 19.6 %collective-permute-done.46 = bf16[128,6144]{1,0:T(8,128)(2,1)S(1)} collective-permute-done((bf16[128,6144]{1,0:T(8,128)(2,1)S(1)}, bf16[128,6144]{1,0:T(8,128)(2,1)S(1)}, u32[]{:S(2)}, u32[]{:S(2)}) %collective-permute-start.46) | collective-permute-done | bytes 1572896 | tf_op jit(solution)/shard_map/ppermute | solution.py:160
  (245 shorter events, 164.3 us)
Async XLA Ops:
  0.0 82.9 %collective-permute-start.13 = (bf16[128,6144]{1,0:T(8,128)(2,1)}, bf16[128,6144]{1,0:T(8,128)(2,1)S(1)}, u32[]{:S(2)}, u32[]{:S(2)}) collective-permute-start(bf16[128,6144]{1,0:T(8,128)(2,1)} %param.7), channel_id=1, source_target_pairs={{0,8},{2,10},{4,12},{6,14},{24,16},{26,18},{28,20},{30,22},{1,9},{... | collective-permute-start | bytes 4718600 | tf_op jit(solution)/shard_map/ppermute | solution.py:160
  6.7 39.1 %collective-permute-start.3 = (bf16[64,6144]{1,0:T(8,128)(2,1)S(1)}, bf16[64,6144]{1,0:T(8,128)(2,1)}, u32[]{:S(2)}, u32[]{:S(2)}) collective-permute-start(bf16[64,6144]{1,0:T(8,128)(2,1)S(1)} %get-tuple-element.91.refs_1_), channel_id=1, source_target_pairs={{0,4},{2,6},{4,0},{6,2},{8,12},{10,14},{12,8},{14,10},{16,20},{18,... | collective-permute-start | bytes 2359304 | tf_op jit(solution)/shard_map/ppermute | solution.py:155
  8.2 40.0 %collective-permute-start.1 = (bf16[64,6144]{1,0:T(8,128)(2,1)S(1)}, bf16[64,6144]{1,0:T(8,128)(2,1)}, u32[]{:S(2)}, u32[]{:S(2)}) collective-permute-start(bf16[64,6144]{1,0:T(8,128)(2,1)S(1)} %get-tuple-element.91.refs_1_), channel_id=1, source_target_pairs={{0,2},{2,0},{4,6},{6,4},{8,10},{10,8},{12,14},{14,12},{16,18},{18,... | collective-permute-start | bytes 2359304 | tf_op jit(solution)/shard_map/ppermute | solution.py:155
  10.3 38.5 %collective-permute-start.2 = (bf16[64,6144]{1,0:T(8,128)(2,1)S(1)}, bf16[64,6144]{1,0:T(8,128)(2,1)}, u32[]{:S(2)}, u32[]{:S(2)}) collective-permute-start(bf16[64,6144]{1,0:T(8,128)(2,1)S(1)} %get-tuple-element.92.refs_0_), channel_id=1, source_target_pairs={{0,4},{2,6},{4,0},{6,2},{8,12},{10,14},{12,8},{14,10},{16,20},{18,... | collective-permute-start | bytes 2359304 | tf_op jit(solution)/shard_map/ppermute | solution.py:155
  43.9 39.7 %collective-permute-start.29 = (bf16[128,6144]{1,0:T(8,128)(2,1)}, bf16[128,6144]{1,0:T(8,128)(2,1)}, u32[]{:S(2)}, u32[]{:S(2)}) collective-permute-start(bf16[128,6144]{1,0:T(8,128)(2,1)} %param.7), channel_id=1, source_target_pairs={{8,16},{10,18},{12,20},{14,22},{16,8},{18,10},{20,12},{22,14},{9,1... | collective-permute-start | bytes 4718600 | tf_op jit(solution)/shard_map/ppermute | solution.py:160
  45.8 39.2 %collective-permute-start.47 = (bf16[128,6144]{1,0:T(8,128)(2,1)}, bf16[128,6144]{1,0:T(8,128)(2,1)}, u32[]{:S(2)}, u32[]{:S(2)}) collective-permute-start(bf16[128,6144]{1,0:T(8,128)(2,1)} %param.7), channel_id=1, source_target_pairs={{8,0},{10,2},{12,4},{14,6},{16,24},{18,26},{20,28},{22,30},{9,1},{... | collective-permute-start | bytes 4718600 | tf_op jit(solution)/shard_map/ppermute | solution.py:160
  83.7 42.5 %collective-permute-start.30 = (bf16[128,6144]{1,0:T(8,128)(2,1)}, bf16[128,6144]{1,0:T(8,128)(2,1)S(1)}, u32[]{:S(2)}, u32[]{:S(2)}) collective-permute-start(bf16[128,6144]{1,0:T(8,128)(2,1)} %collective-permute-done.29), channel_id=1, source_target_pairs={{8,0},{10,2},{12,4},{14,6},{16,24},{18,26},{20,28},{22,30},{9,1},{... | collective-permute-start | bytes 4718600 | tf_op jit(solution)/shard_map/ppermute | solution.py:160
  90.0 37.8 %collective-permute-start.49 = (bf16[64,6144]{1,0:T(8,128)(2,1)S(1)}, bf16[64,6144]{1,0:T(8,128)(2,1)}, u32[]{:S(2)}, u32[]{:S(2)}) collective-permute-start(bf16[64,6144]{1,0:T(8,128)(2,1)S(1)} %get-tuple-element.89.refs_1_), channel_id=1, source_target_pairs={{0,2},{2,0},{4,6},{6,4},{8,10},{10,8},{12,14},{14,12},{16,18},{18,... | collective-permute-start | bytes 2359304 | tf_op jit(solution)/shard_map/ppermute | solution.py:155
  127.8 56.6 %collective-permute-start.34 = (bf16[64,6144]{1,0:T(8,128)(2,1)S(1)}, bf16[64,6144]{1,0:T(8,128)(2,1)}, u32[]{:S(2)}, u32[]{:S(2)}) collective-permute-start(bf16[64,6144]{1,0:T(8,128)(2,1)S(1)} %get-tuple-element.87.refs_1_), channel_id=1, source_target_pairs={{0,4},{2,6},{4,0},{6,2},{8,12},{10,14},{12,8},{14,10},{16,20},{18,... | collective-permute-start | bytes 2359304 | tf_op jit(solution)/shard_map/ppermute | solution.py:155
  128.4 74.5 %collective-permute-start.32 = (bf16[64,6144]{1,0:T(8,128)(2,1)S(1)}, bf16[64,6144]{1,0:T(8,128)(2,1)}, u32[]{:S(2)}, u32[]{:S(2)}) collective-permute-start(bf16[64,6144]{1,0:T(8,128)(2,1)S(1)} %get-tuple-element.87.refs_1_), channel_id=1, source_target_pairs={{0,2},{2,0},{4,6},{6,4},{8,10},{10,8},{12,14},{14,12},{16,18},{18,... | collective-permute-start | bytes 2359304 | tf_op jit(solution)/shard_map/ppermute | solution.py:155
  204.7 40.8 %collective-permute-start.56 = (bf16[64,6144]{1,0:T(8,128)(2,1)}, bf16[64,6144]{1,0:T(8,128)(2,1)S(1)}, u32[]{:S(2)}, u32[]{:S(2)}) collective-permute-start(bf16[64,6144]{1,0:T(8,128)(2,1)} %get-tuple-element.80), channel_id=1, source_target_pairs={{0,4},{2,6},{4,0},{6,2},{8,12},{10,14},{12,8},{14,10},{16,20},{18,... | collective-permute-start | bytes 2359304 | tf_op jit(solution)/shard_map/ppermute | solution.py:155
  211.8 38.7 %collective-permute-start.17 = (bf16[64,6144]{1,0:T(8,128)(2,1)S(1)}, bf16[64,6144]{1,0:T(8,128)(2,1)S(1)}, u32[]{:S(2)}, u32[]{:S(2)}) collective-permute-start(bf16[64,6144]{1,0:T(8,128)(2,1)S(1)} %get-tuple-element.85.refs_1_), channel_id=1, source_target_pairs={{0,2},{2,0},{4,6},{6,4},{8,10},{10,8},{12,14},{14,12},{16,18},{18,... | collective-permute-start | bytes 2359304 | tf_op jit(solution)/shard_map/ppermute | solution.py:155
  221.2 41.2 %collective-permute-start.18 = (bf16[64,6144]{1,0:T(8,128)(2,1)S(1)}, bf16[64,6144]{1,0:T(8,128)(2,1)}, u32[]{:S(2)}, u32[]{:S(2)}) collective-permute-start(bf16[64,6144]{1,0:T(8,128)(2,1)S(1)} %get-tuple-element.86.refs_0_), channel_id=1, source_target_pairs={{0,4},{2,6},{4,0},{6,2},{8,12},{10,14},{12,8},{14,10},{16,20},{18,... | collective-permute-start | bytes 2359304 | tf_op jit(solution)/shard_map/ppermute | solution.py:155
  238.2 59.0 %collective-permute-start.37 = (bf16[48,128,128]{2,1,0:T(8,128)(2,1)}, bf16[48,128,128]{2,1,0:T(8,128)(2,1)S(1)}, u32[]{:S(2)}, u32[]{:S(2)}) collective-permute-start(bf16[48,128,128]{2,1,0:T(8,128)(2,1)} %get-tuple-element.66), channel_id=1, source_target_pairs={{0,1},{1,0},{2,3},{3,2},{4,5},{5,4},{6,7},{7,6},{8,9},{9,8},{10,11... | collective-permute-start | bytes 4718600 | tf_op jit(solution)/shard_map/ppermute | solution.py:242
  238.3 40.9 %collective-permute-start.20 = (bf16[64,6144]{1,0:T(8,128)(2,1)}, bf16[64,6144]{1,0:T(8,128)(2,1)S(1)}, u32[]{:S(2)}, u32[]{:S(2)}) collective-permute-start(bf16[64,6144]{1,0:T(8,128)(2,1)} %collective-permute-done.16.refs_2_), channel_id=1, source_target_pairs={{0,4},{2,6},{4,0},{6,2},{8,12},{10,14},{12,8},{14,10},{16,20},{18,... | collective-permute-start | bytes 2359304 | tf_op jit(solution)/shard_map/ppermute | solution.py:155
  250.6 288.0 %collective-permute-start.7 = (bf16[64,6144]{1,0:T(8,128)(2,1)}, bf16[64,6144]{1,0:T(8,128)(2,1)S(1)}, u32[]{:S(2)}, u32[]{:S(2)}) collective-permute-start(bf16[64,6144]{1,0:T(8,128)(2,1)} %get-tuple-element.48), channel_id=1, source_target_pairs={{0,4},{2,6},{4,0},{6,2},{8,12},{10,14},{12,8},{14,10},{16,20},{18,... | collective-permute-start | bytes 2359304 | tf_op jit(solution)/shard_map/ppermute | solution.py:155
  262.5 291.2 %collective-permute-start.10 = (bf16[64,6144]{1,0:T(8,128)(2,1)}, bf16[64,6144]{1,0:T(8,128)(2,1)S(1)}, u32[]{:S(2)}, u32[]{:S(2)}) collective-permute-start(bf16[64,6144]{1,0:T(8,128)(2,1)} %get-tuple-element.52), channel_id=1, source_target_pairs={{0,2},{2,0},{4,6},{6,4},{8,10},{10,8},{12,14},{14,12},{16,18},{18,... | collective-permute-start | bytes 2359304 | tf_op jit(solution)/shard_map/ppermute | solution.py:155
  297.1 38.1 %collective-permute-start.22 = (bf16[48,128,128]{2,1,0:T(8,128)(2,1)}, bf16[48,128,128]{2,1,0:T(8,128)(2,1)S(1)}, u32[]{:S(2)}, u32[]{:S(2)}) collective-permute-start(bf16[48,128,128]{2,1,0:T(8,128)(2,1)} %get-tuple-element.56), channel_id=1, source_target_pairs={{0,1},{1,0},{2,3},{3,2},{4,5},{5,4},{6,7},{7,6},{8,9},{9,8},{10,11... | collective-permute-start | bytes 4718600 | tf_op jit(solution)/shard_map/ppermute | solution.py:242
  315.6 111.8 %collective-permute-start.38 = (bf16[64,6144]{1,0:T(8,128)(2,1)}, bf16[64,6144]{1,0:T(8,128)(2,1)}, u32[]{:S(2)}, u32[]{:S(2)}) collective-permute-start(bf16[64,6144]{1,0:T(8,128)(2,1)} %get-tuple-element.68), channel_id=1, source_target_pairs={{0,4},{2,6},{4,0},{6,2},{8,12},{10,14},{12,8},{14,10},{16,20},{18,... | collective-permute-start | bytes 2359304 | tf_op jit(solution)/shard_map/ppermute | solution.py:155
  353.6 38.4 %collective-permute-start.23 = (bf16[64,6144]{1,0:T(8,128)(2,1)S(1)}, bf16[64,6144]{1,0:T(8,128)(2,1)S(1)}, u32[]{:S(2)}, u32[]{:S(2)}) collective-permute-start(bf16[64,6144]{1,0:T(8,128)(2,1)S(1)} %copy-done.43), channel_id=1, source_target_pairs={{0,4},{2,6},{4,0},{6,2},{8,12},{10,14},{12,8},{14,10},{16,20},{18,... | collective-permute-start | bytes 2359304 | tf_op jit(solution)/shard_map/ppermute | solution.py:155
  424.8 40.4 %collective-permute-start.41 = (bf16[64,6144]{1,0:T(8,128)(2,1)S(1)}, bf16[64,6144]{1,0:T(8,128)(2,1)S(1)}, u32[]{:S(2)}, u32[]{:S(2)}) collective-permute-start(bf16[64,6144]{1,0:T(8,128)(2,1)S(1)} %copy-done.41), channel_id=1, source_target_pairs={{0,2},{2,0},{4,6},{6,4},{8,10},{10,8},{12,14},{14,12},{16,18},{18,... | collective-permute-start | bytes 2359304 | tf_op jit(solution)/shard_map/ppermute | solution.py:155
  427.4 40.0 %collective-permute-start.43 = (bf16[64,6144]{1,0:T(8,128)(2,1)S(1)}, bf16[64,6144]{1,0:T(8,128)(2,1)S(1)}, u32[]{:S(2)}, u32[]{:S(2)}) collective-permute-start(bf16[64,6144]{1,0:T(8,128)(2,1)S(1)} %add_convert_fusion.3), channel_id=1, source_target_pairs={{0,4},{2,6},{4,0},{6,2},{8,12},{10,14},{12,8},{14,10},{16,20},{18,... | collective-permute-start | bytes 2359304 | tf_op jit(solution)/shard_map/ppermute | solution.py:155
  467.3 43.8 %collective-permute-start.58 = (bf16[64,6144]{1,0:T(8,128)(2,1)S(1)}, bf16[64,6144]{1,0:T(8,128)(2,1)S(1)}, u32[]{:S(2)}, u32[]{:S(2)}) collective-permute-start(bf16[64,6144]{1,0:T(8,128)(2,1)S(1)} %copy-done.39), channel_id=1, source_target_pairs={{0,2},{2,0},{4,6},{6,4},{8,10},{10,8},{12,14},{14,12},{16,18},{18,... | collective-permute-start | bytes 2359304 | tf_op jit(solution)/shard_map/ppermute | solution.py:155
  511.9 40.1 %collective-permute-start.9 = (bf16[64,6144]{1,0:T(8,128)(2,1)S(1)}, bf16[64,6144]{1,0:T(8,128)(2,1)S(1)}, u32[]{:S(2)}, u32[]{:S(2)}) collective-permute-start(bf16[64,6144]{1,0:T(8,128)(2,1)S(1)} %copy-done.12), channel_id=1, source_target_pairs={{0,2},{2,0},{4,6},{6,4},{8,10},{10,8},{12,14},{14,12},{16,18},{18,... | collective-permute-start | bytes 2359304 | tf_op jit(solution)/shard_map/ppermute | solution.py:155
  (85 other events, 1873.0 us)

commit v2 on v0

--- a/solution.py
+++ b/solution.py
@@ -1,13 +1,365 @@
+import functools
+
 import jax
 import jax.numpy as jnp
 from jax import lax
+from jax.experimental import pallas as pl
+from jax.experimental.pallas import tpu as pltpu
 from jax.sharding import PartitionSpec as P
 
 BLK = 128
 K = 48
-
-
-def per_device(tokens, active, w_up, b_up, w_down, b_down):
+HALF = BLK // 2
+PLANE = 4
+LAYERS = 4
+DEPTH = 3
+VMEM_BYTES = 56 * 1024 * 1024
+
+
+def stream(meta, count, copies_of, ready, use):
+    def each(step, slot, act):
+        for copy, wanted in copies_of(step, slot):
+            if wanted is None:
+                act(copy)
+            else:
+                pl.when(wanted)(functools.partial(act, copy))
+
+    def start(step, slot):
+        each(step, slot, lambda copy: copy.start())
+
+    for ahead in range(DEPTH - 1):
+        @pl.when(ahead < count)
+        def _():
+            start(ahead, ahead)
+
+    ready()
+
+    def body(step, carry):
+        nearest = step + DEPTH - 1
+
+        @pl.when(nearest < count)
+        def _():
+            start(nearest, lax.rem(nearest, DEPTH))
+
+        slot = lax.rem(step, DEPTH)
+        each(step, slot, lambda copy: copy.wait())
+        use(step, slot)
+        return carry
+
+    lax.fori_loop(0, count, body, 0)
+
+
+def up_kernel(per_owner, meta, *refs):
+    parts, refs = refs[:PLANE + 1], refs[PLANE + 1:]
+    w_ref, own_ref, send_ref, rows, held, own, send, row_sems, sems, own_sems, send_sems = refs
+    count = meta[0]
+    places = [rows.at[0], rows.at[1], rows.at[2], rows.at[3, pl.ds(0, HALF)], rows.at[3, pl.ds(HALF, HALF)]]
+    copies = [pltpu.make_async_copy(*ends, row_sems.at[at]) for at, ends in enumerate(zip(parts, places))]
+    for copy in copies:
+        copy.start()
+
+    def ready():
+        for copy in copies:
+            copy.wait()
+
+    def copies_of(step, slot):
+        for side in range(2):
+            code = meta[1 + 2 * step + side]
+            block = lax.rem(jnp.maximum(code, 0), per_owner)
+            cols = pl.ds(pl.multiple_of(block * BLK, BLK), BLK)
+            place = held.at[slot, :, pl.ds(side * BLK, BLK)]
+            yield pltpu.make_async_copy(w_ref.at[:, cols], place, sems.at[slot, side]), code >= 0 if side else None
+
+    def results(step):
+        slot = lax.rem(step, 2)
+        pair = pl.ds(2 * step, 2)
+        return (pltpu.make_async_copy(own.at[slot], own_ref.at[pair], own_sems.at[slot]),
+                pltpu.make_async_copy(send.at[slot], send_ref.at[pair], send_sems.at[slot]))
+
+    def use(step, slot):
+        offset = lax.div(meta[1 + 2 * step], per_owner)
+        preact = jnp.dot(rows[offset], held[slot], preferred_element_type=jnp.float32)
+
+        @pl.when(step >= 2)
+        def _():
+            for copy in results(step - 2):
+                copy.wait()
+
+        at = lax.rem(step, 2)
+        for side in range(2):
+            cols = slice(side * BLK, (side + 1) * BLK)
+            own[at, side] = preact[:, cols]
+            send[at, side] = preact[:, cols].astype(jnp.bfloat16)
+        for copy in results(step):
+            copy.start()
+
+    stream(meta, count, copies_of, ready, use)
+    for back in (2, 1):
+        @pl.when(count >= back)
+        def _():
+            for copy in results(count - back):
+                copy.wait()
+
+
+def estimate(feat):
+    return pl.CostEstimate(flops=2 * BLK * BLK * feat, bytes_accessed=BLK * feat * 2, transcendentals=0)
+
+
+def up_group(meta, parts, w_up, slots):
+    feat = w_up.shape[0]
+    per_owner = w_up.shape[1] // BLK
+    anywhere = pl.BlockSpec(memory_space=pl.ANY)
+    return pl.pallas_call(
+        functools.partial(up_kernel, per_owner),
+        in_specs=[pl.BlockSpec(memory_space=pltpu.SMEM)] + [anywhere] * (len(parts) + 1),
+        out_specs=[anywhere] * 2,
+        scratch_shapes=[
+            pltpu.VMEM((PLANE, BLK, feat), jnp.bfloat16),
+            pltpu.VMEM((DEPTH, feat, 2 * BLK), jnp.bfloat16),
+            pltpu.VMEM((2, 2, BLK, BLK), jnp.float32),
+            pltpu.VMEM((2, 2, BLK, BLK), jnp.bfloat16),
+            pltpu.SemaphoreType.DMA((len(parts),)),
+            pltpu.SemaphoreType.DMA((DEPTH, 2)),
+            pltpu.SemaphoreType.DMA((2,)),
+            pltpu.SemaphoreType.DMA((2,)),
+        ],
+        out_shape=[
+            jax.ShapeDtypeStruct((slots, BLK, BLK), jnp.float32),
+            jax.ShapeDtypeStruct((slots, BLK, BLK), jnp.bfloat16),
+        ],
+        compiler_params=pltpu.CompilerParams(vmem_limit_bytes=VMEM_BYTES),
+        cost_estimate=estimate(feat),
+        name="up_group",
+    )(meta, *parts, w_up)
+
+
+def down_kernel(per_owner, slots, meta, own_ref, other_ref, bias_ref, w_ref, *refs):
+    outs, (total, held, own, other, done, sems, done_sems) = refs[:PLANE + 1], refs[PLANE + 1:]
+    count = meta[0]
+    width = total.shape[1]
+    piece = width // 6 if width % (6 * BLK) == 0 else width
+
+    def results(o):
+        if o < PLANE - 1:
+            return [pltpu.make_async_copy(done.at[o], outs[o], done_sems.at[o])]
+        halves = [pl.ds(0, HALF), pl.ds(HALF, HALF)]
+        return [pltpu.make_async_copy(done.at[o, half], outs[o + at], done_sems.at[o + at]) for at, half in enumerate(halves)]
+
+    def copies_of(step, slot):
+        pair = pl.ds(2 * step, 2)
+        yield pltpu.make_async_copy(own_ref.at[pair], own.at[slot], sems.at[slot, 2]), None
+        yield pltpu.make_async_copy(other_ref.at[pair], other.at[slot], sems.at[slot, 3]), None
+        left, right = meta[1 + 2 * step], meta[2 + 2 * step]
+        for side, code in enumerate((left, jnp.where(right < 0, left, right))):
+            rows = pl.ds(pl.multiple_of(lax.rem(code, per_owner) * BLK, BLK), BLK)
+            place = held.at[slot, pl.ds(side * BLK, BLK)]
+            yield pltpu.make_async_copy(w_ref.at[rows], place, sems.at[slot, side]), None
+
+    def hidden_of(slot, side, code):
+        preact = own[slot, side] + other[slot, side].astype(jnp.float32) + bias_ref[lax.rem(code, per_owner)]
+        return jnp.maximum(preact, 0.0)
+
+    def use(step, slot):
+        left, right = meta[1 + 2 * step], meta[2 + 2 * step]
+        offset = lax.div(left, per_owner)
+        before = lax.div(meta[jnp.maximum(2 * step - 1, 1)], per_owner)
+        after = lax.div(meta[3 + 2 * step], per_owner)
+        first = (step == 0) | (before != offset)
+        last = (step >= count - 1) | (after != offset)
+        one = hidden_of(slot, 0, left)
+        two = jnp.where(right < 0, 0.0, hidden_of(slot, 1, jnp.maximum(right, 0)))
+        hidden = jnp.concatenate([one, two], axis=1).astype(jnp.bfloat16)
+        for at in range(0, width, piece):
+            cols = pl.ds(at, piece)
+            term = jnp.dot(hidden, held[slot, :, cols], preferred_element_type=jnp.float32)
+            total[:, cols] = jnp.where(first, 0.0, total[:, cols]) + term
+
+        @pl.when(last)
+        def _():
+            done[offset] = total[...].astype(jnp.bfloat16)
+
+        for o in range(PLANE):
+            @pl.when(last & (offset == o))
+            def _():
+                for copy in results(o):
+                    copy.start()
+
+    stream(meta, count, copies_of, lambda: None, use)
+    for o in range(PLANE):
+        @pl.when(meta[1 + slots + 2 + o] == 0)
+        def _():
+            done[o] = jnp.zeros_like(done[o])
+            for copy in results(o):
+                copy.start()
+
+    for o in range(PLANE):
+        for copy in results(o):
+            copy.wait()
+
+
+def down_group(meta, own, other, bias, w_down):
+    feat = w_down.shape[1]
+    per_owner = w_down.shape[0] // BLK
+    anywhere = pl.BlockSpec(memory_space=pl.ANY)
+    whole = pl.BlockSpec(memory_space=pltpu.VMEM)
+    return pl.pallas_call(
+        functools.partial(down_kernel, per_owner, own.shape[0]),
+        in_specs=[pl.BlockSpec(memory_space=pltpu.SMEM), anywhere, anywhere, whole, anywhere],
+        out_specs=[anywhere] * (PLANE + 1),
+        scratch_shapes=[
+            pltpu.VMEM((BLK, feat), jnp.float32),
+            pltpu.VMEM((DEPTH, 2 * BLK, feat), jnp.bfloat16),
+            pltpu.VMEM((DEPTH, 2, BLK, BLK), jnp.float32),
+            pltpu.VMEM((DEPTH, 2, BLK, BLK), jnp.bfloat16),
+            pltpu.VMEM((PLANE, BLK, feat), jnp.bfloat16),
+            pltpu.SemaphoreType.DMA((DEPTH, 4)),
+            pltpu.SemaphoreType.DMA((PLANE + 1,)),
+        ],
+        out_shape=[jax.ShapeDtypeStruct((rows, feat), jnp.bfloat16) for rows in (BLK, BLK, BLK, HALF, HALF)],
+        compiler_params=pltpu.CompilerParams(vmem_limit_bytes=VMEM_BYTES),
+        cost_estimate=estimate(feat),
+        name="down_group",
+    )(meta, own, other, bias, w_down)
+
+
+def add_kernel(x_ref, y_ref, x_add, y_add, x_out, y_out):
+    x_out[...] = (x_ref[...].astype(jnp.float32) + x_add[...].astype(jnp.float32)).astype(jnp.bfloat16)
+    y_out[...] = (y_ref[...].astype(jnp.float32) + y_add[...].astype(jnp.float32)).astype(jnp.bfloat16)
+
+
+def add_diagonal(over_x, over_y, x_add, y_add):
+    feat = over_x.shape[1]
+    steps = 3
+    upper = pl.BlockSpec((HALF, feat // steps), lambda i: (0, i))
+    lower = pl.BlockSpec((HALF, feat // steps), lambda i: (1, i))
+    return pl.pallas_call(
+        add_kernel,
+        grid=(steps,),
+        in_specs=[upper, lower, upper, upper],
+        out_specs=[upper, lower],
+        out_shape=[jax.ShapeDtypeStruct(over_x.shape, jnp.bfloat16)] * 2,
+        input_output_aliases={0: 0, 1: 1},
+        name="add_diagonal",
+    )(over_x, over_y, x_add, y_add)
+
+
+def swap(value, bits):
+    return lax.ppermute(value, "wa", [(w, w ^ bits) for w in range(LAYERS * PLANE)])
+
+
+def add(*terms):
+    total = terms[0].astype(jnp.float32)
+    for term in terms[1:]:
+        total = total + term.astype(jnp.float32)
+    return total
+
+
+def narrow(*terms):
+    return add(*terms).astype(jnp.bfloat16)
+
+
+def pair_lists(active, owner, per_owner):
+    layer, cell = owner // PLANE, owner % PLANE
+    order = jnp.array([[0, 1, 2, 3], [1, 0, 2, 3], [2, 3, 1, 0], [3, 2, 1, 0]], jnp.int32)
+    layers = jnp.sum(jnp.where(jnp.arange(LAYERS)[:, None] == layer, order, 0), axis=0)
+    blocks = layers[:, None] * PLANE + (cell ^ jnp.arange(PLANE, dtype=jnp.int32))[None, :]
+    targets = owner * per_owner + jnp.arange(per_owner, dtype=jnp.int32)
+    hits = jnp.any(active[:, :, None] == targets[None, None, :], axis=1)
+    is_block = blocks[:, :, None] == jnp.arange(active.shape[0], dtype=jnp.int32)
+    hits = jnp.any(is_block[..., None] & hits[None, None], axis=2).astype(jnp.int32)
+    counts = jnp.sum(hits, axis=2)
+    padded = counts + counts % 2
+    starts = jnp.cumsum(padded, axis=1) - padded
+    number = (starts[:, :, None] + jnp.cumsum(hits, axis=2)) * hits
+    number = number.reshape(LAYERS, PLANE * per_owner)
+    slots = 2 * per_owner + PLANE
+    codes = jnp.arange(PLANE * per_owner, dtype=jnp.int32) + 1
+    wanted = jnp.arange(slots, dtype=jnp.int32) + 1
+    lists = jnp.sum(jnp.where(number[:, :, None] == wanted, codes[None, :, None], 0), axis=1) - 1
+    steps = jnp.sum(padded, axis=1, keepdims=True) // 2
+    return jnp.concatenate([steps, lists, jnp.full((LAYERS, 2), -1, jnp.int32), counts], axis=1), slots
+
+
+def along_z(value, *hops):
+    pairs = [(a * PLANE + q, b * PLANE + q) for a, b in hops for q in range(PLANE)]
+    return lax.ppermute(value, "wa", pairs)
+
+
+def together(*values):
+    return lax.optimization_barrier(values)
+
+
+def sides(block):
+    return swap(block, 1), swap(block, 2)
+
+
+def sides2(blocks):
+    return swap(blocks[0], 1), swap(blocks[1], 2)
+
+
+def corner(over_x, over_y):
+    return swap(over_x[:HALF], 2), swap(over_y[HALF:], 1)
+
+
+def by_layers(tokens, active, w_up, b_up, w_down, b_down):
+    per_owner = w_up.shape[1] // BLK
+    owner = lax.axis_index("wa")
+    inner = (owner // PLANE == 1) | (owner // PLANE == 2)
+    meta, slots = pair_lists(active, owner, per_owner)
+    bias = b_up.reshape(per_owner, 1, BLK)
+
+    def up(at, block, side, diagonal):
+        return up_group(meta[at], [block, *side, *diagonal], w_up, slots)
+
+    def down(at, sums):
+        other = lax.ppermute(sums[1], "row", [(0, 1), (1, 0)])
+        return down_group(meta[at], sums[0], other, bias, w_down)
+
+    def cross(partial):
+        return swap(partial[3], 2), swap(partial[4], 1)
+
+    def summed(partial, crossed):
+        return add_diagonal(partial[1], partial[2], *crossed)
+
+    near, middle, side0 = swap(tokens, PLANE), along_z(tokens, (1, 2), (2, 1)), sides(tokens)
+    near, middle, side0 = together(near, middle, side0)
+    diag0, side1 = corner(*side0), sides(near)
+    across, outward = along_z(near, (1, 2), (2, 1)), along_z(middle, (1, 0), (2, 3))
+    across, outward, side1, diag0 = together(across, outward, side1, diag0)
+    far = jnp.where(inner, middle, outward)
+    diag1, side2, outward = corner(*side1), sides(far), along_z(across, (1, 0), (2, 3))
+    up0 = up(0, tokens, side0, diag0)
+    outward, side2, diag1, up0 = together(outward, side2, diag1, up0)
+    last = jnp.where(inner, across, outward)
+    diag2, side3 = corner(*side2), sides(last)
+    part0, up1 = down(0, up0), up(1, near, side1, diag1)
+    side3, diag2, part0, up1 = together(side3, diag2, part0, up1)
+    diag3, cross0 = corner(*side3), cross(part0)
+    part1, up2 = down(1, up1), up(2, far, side2, diag2)
+    up3 = up(3, last, side3, diag3)
+    cross0, part1, up2, up3 = together(cross0, part1, up2, up3)
+    cross1, part2, part3 = cross(part1), down(2, up2), down(3, up3)
+    cross1, part2, part3 = together(cross1, part2, part3)
+    cross3, cross2 = cross(part3), cross(part2)
+    sent3 = summed(part3, cross3)
+    sent3, cross2, part1, cross1, part0, cross0 = together(sent3, cross2, part1, cross1, part0, cross0)
+    got3 = sides2(sent3)
+    sent2 = summed(part2, cross2)
+    got2 = sides2(sent2)
+    sum3 = narrow(part3[0], *got3)
+    passed = along_z(sum3, (0, 1), (3, 2))
+    sent1, sent0 = summed(part1, cross1), summed(part0, cross0)
+    got2, sum3, sent1, sent0 = together(got2, sum3, sent1, sent0)
+    got1, got0 = sides2(sent1), sides2(sent0)
+    sum2 = narrow(part2[0], *got2)
+    passed = along_z(narrow(sum3, passed), (1, 2), (2, 1))
+    inward = along_z(sum2, (0, 1), (3, 2))
+    near = swap(narrow(part1[0], passed, *got1), PLANE)
+    middle = along_z(narrow(sum2, inward), (1, 2), (2, 1))
+    return (add(part0[0], *got0, near, middle) + b_down).astype(jnp.bfloat16)
+
+
+def general(tokens, active, w_up, b_up, w_down, b_down):
     feat_dev = tokens.shape[1]
     tblocks = active.shape[0]
     owners = lax.axis_size("wa")
@@ -35,15 +387,14 @@
     contrib = contrib.reshape(per_owner, capacity, BLK, feat_dev)
     placing = picked.transpose(1, 2, 0).astype(jnp.float32)
     partial_value = jnp.einsum("jct,jcqd->tqd", placing, contrib, precision=lax.Precision.HIGHEST)
-    partial_value = partial_value.astype(jnp.bfloat16)
-    terms = partial_value.reshape(tblocks * BLK, feat_dev).astype(jnp.float32)
-    total = lax.psum_scatter(
-        terms.astype(jnp.bfloat16), "wa", scatter_dimension=0, tiled=True
-    ).astype(jnp.float32)
+    terms = partial_value.reshape(tblocks * BLK, feat_dev).astype(jnp.bfloat16)
+    total = lax.psum_scatter(terms, "wa", scatter_dimension=0, tiled=True).astype(jnp.float32)
     return (total + b_down).astype(jnp.bfloat16)
 
 
 def solution(mesh):
+    sizes = (mesh.shape["wa"], mesh.shape["row"])
+    per_device = by_layers if sizes == (LAYERS * PLANE, 2) else general
     in_specs = (P("wa", "row"), P(), P("row", "wa"), P("wa"), P("wa", "row"), P("row"))
     out_specs = P("wa", "row")
     return jax.shard_map(

time: 1030 us -> 488 us (0.47)
  waiting for transfers between devices: 658 us -> 270 us
  matrix products: 292 us -> 0 us
  Pallas kernels: 0 us -> 120 us
  starting transfers between devices: 0.08 us -> 57.6 us
  local copies, waits for them, and re-layouts: 60.4 us -> 21.2 us
  other arithmetic: 4.12 us -> 17.4 us
  between operations: 13.2 us -> 0.65 us
    reduce_scatter x1 -> x0, waiting for transfers between devices: 363 us -> none  [per_device(): lax.psum_scatter(terms.astype(jnp.bfloat16), 'wa', scatter_dimension=0, t...]
    dot_general x3 -> x0, matrix products: 292 us -> none  [the longest x1 189 us: per_device(): jnp.einsum('jct,jcqd->tqd', placing, contrib, precision=lax.Precision.HIG...]
    all_gather x1 -> x0, waiting for transfers between devices: 275 us -> none  [per_device(): gathered = lax.all_gather(tokens, 'wa', axis=0, tiled=True)]
    ppermute x0 -> x46, waiting for transfers between devices: none -> 270 us  [the longest x34 243 us: swap(): lax.ppermute(value, 'wa', [(w, w ^ bits) for w in range(LAYERS * PLANE)])]
    pallas_call x0 -> x12, Pallas kernels: none -> 120 us  [the longest x4 59.2 us: down_group(): pl.pallas_call(functools.partial(down_kernel, per_owner, own.shape[0]), i...]
    ppermute x0 -> x46, starting transfers between devices: none -> 57.6 us  [the longest x34 37.3 us: swap(): lax.ppermute(value, 'wa', [(w, w ^ bits) for w in range(LAYERS * PLANE)])]
    gather x1 -> x0, local copies, waits for them, and re-layouts: 33.4 us -> none  [per_device(): token_blocks[slot_tok.reshape(-1)]]
    convert_element_type x1 -> x0, local copies, waits for them, and re-layouts: 26.8 us -> none  [per_device(): partial_value = partial_value.astype(jnp.bfloat16)]
  transfers between devices with their start and end apart: 3 -> 46, of which waited for: 3 -> 22; matrix products, arithmetic and copies ran while one was open for 0% -> 4% of each run, Pallas kernels for 0% -> 25%
where the time goes in v2:
time: 488 us; the launch traced here: 487 us
  waiting for transfers between devices  270 us (55%)
  Pallas kernels  120 us (25%)
  starting transfers between devices  57.6 us (12%)
  local copies, waits for them, and re-layouts  21.2 us (4%)
  other arithmetic  17.4 us (4%)
    ppermute x34, waiting for transfers between devices, swap(): lax.ppermute(value, 'wa', [(w, w ^ bits) for w in range(LAYERS * PLANE)])  243 us
    pallas_call x4, Pallas kernels, down_group(): pl.pallas_call(functools.partial(down_kernel, per_owner, own.shape[0]), i...  59.2 us
    pallas_call x4, Pallas kernels, up_group(): pl.pallas_call(functools.partial(up_kernel, per_owner), in_specs=[pl.Bloc...  46.2 us
    ppermute x34, starting transfers between devices, swap(): lax.ppermute(value, 'wa', [(w, w ^ bits) for w in range(LAYERS * PLANE)])  37.3 us
    ppermute x8, waiting for transfers between devices, along_z(): return lax.ppermute(value, 'wa', pairs)  25.9 us
    ppermute x8, starting transfers between devices, along_z(): return lax.ppermute(value, 'wa', pairs)  19.7 us
    pallas_call x4, Pallas kernels, add_diagonal(): pl.pallas_call(add_kernel, grid=(steps,), in_specs=[upper, lower, upper,...  15.1 us
    unnamed x76, local copies, waits for them, and re-layouts  14.7 us
  transfers between devices with their start and end apart: 46, of which 22 were waited for; matrix products, arithmetic and copies ran while one was open for 4% of the time, Pallas kernels for 25%

profile of v2, /device:TPU:0, one launch (start us, length us, event | category | flops | bytes accessed | tf_op | source)
XLA Modules:
  0.0 487.3 jit_solution(9724918660514459498)
XLA Ops:
  7.9 29.9 %collective-permute-done.refs_0_ = bf16[128,6144]{1,0:T(8,128)(2,1)} collective-permute-done((bf16[128,6144]{1,0:T(8,128)(2,1)}, bf16[128,6144]{1,0:T(8,128)(2,1)}, u32[]{:S(2)}, u32[]{:S(2)}) %collective-permute-start) | collective-permute-done | bytes 1572896 | tf_op jit(solution)/shard_map/ppermute | solution.py:247
  50.3 13.7 %collective-permute-done.8.refs_3_ = bf16[64,6144]{1,0:T(8,128)(2,1)} collective-permute-done((bf16[64,6144]{1,0:T(8,128)(2,1)}, bf16[64,6144]{1,0:T(8,128)(2,1)}, u32[]{:S(2)}, u32[]{:S(2)}) %collective-permute-start.8) | collective-permute-done | bytes 786464 | tf_op jit(solution)/shard_map/ppermute | solution.py:247
  65.4 32.5 %collective-permute-done.9.refs_4_ = bf16[64,6144]{1,0:T(8,128)(2,1)S(1)} collective-permute-done((bf16[64,6144]{1,0:T(8,128)(2,1)S(1)}, bf16[64,6144]{1,0:T(8,128)(2,1)S(1)}, u32[]{:S(2)}, u32[]{:S(2)}) %collective-permute-start.9) | collective-permute-done | bytes 786464 | tf_op jit(solution)/shard_map/ppermute | solution.py:247
  111.4 11.5 %up_group.4 = (f32[52,128,128]{2,1,0:T(8,128)}, bf16[52,128,128]{2,1,0:T(8,128)(2,1)}) custom-call(s32[59]{0:T(128)} %get-tuple-element.226.meta, bf16[128,6144]{1,0:T(8,128)(2,1)} %refs_0_.1, bf16[128,6144]{1,0:T(8,128)(2,1)} %copy-done.5, bf16[128,6144]{1,0:T(8,128)(2,1)} %collective-permute-done.3.refs_2_, ...), custom_call_target="tpu_custom_call" | custom-call | flops 201326592 | bytes 1572864 | tf_op jit(solution)/shard_map/up_group/pallas_call | solution.py:112
  122.9 29.5 %collective-permute-done.13.refs_3_ = bf16[64,6144]{1,0:T(8,128)(2,1)S(1)} collective-permute-done((bf16[64,6144]{1,0:T(8,128)(2,1)}, bf16[64,6144]{1,0:T(8,128)(2,1)S(1)}, u32[]{:S(2)}, u32[]{:S(2)}) %collective-permute-start.13) | collective-permute-done | bytes 786464 | tf_op jit(solution)/shard_map/ppermute | solution.py:247
  161.5 11.5 %up_group.5 = (f32[52,128,128]{2,1,0:T(8,128)}, bf16[52,128,128]{2,1,0:T(8,128)(2,1)}) custom-call(s32[59]{0:T(128)} %get-tuple-element.225.meta, bf16[128,6144]{1,0:T(8,128)(2,1)} %collective-permute-done.refs_0_, bf16[128,6144]{1,0:T(8,128)(2,1)} %copy-done.2, bf16[128,6144]{1,0:T(8,128)(2,1)} %copy-done.3, bf16[64,6144]{1,0:T(8,128)(2,1)} %copy-done.28, ...), custom_call_target="tpu_custom_call" | custom-call | flops 201326592 | bytes 1572864 | tf_op jit(solution)/shard_map/up_group/pallas_call | solution.py:112
  174.3 14.9 %down_group.4 = (bf16[128,6144]{1,0:T(8,128)(2,1)}, bf16[128,6144]{1,0:T(8,128)(2,1)}, bf16[128,6144]{1,0:T(8,128)(2,1)}, bf16[64,6144]{1,0:T(8,128)(2,1)}, bf16[64,6144]{1,0:T(8,128)(2,1)}) custom-call(s32[59]{0:T(128)} %get-tuple-element.226.meta, f32[52,128,128]{2,1,0:T(8,128)} %get-tuple-element.128.own_ref, bf16[52,128,128]{2,1,0:T(8,128)(2,1)} %copy-done.9, ...), custom_call_target="tpu_custom_call" | custom-call | flops 201326592 | bytes 1572864 | tf_op jit(solution)/shard_map/down_group/pallas_call | solution.py:205
  189.2 20.6 %collective-permute-done.17.refs_3_ = bf16[64,6144]{1,0:T(8,128)(2,1)} collective-permute-done((bf16[64,6144]{1,0:T(8,128)(2,1)S(1)}, bf16[64,6144]{1,0:T(8,128)(2,1)}, u32[]{:S(2)}, u32[]{:S(2)}) %collective-permute-start.17) | collective-permute-done | bytes 786464 | tf_op jit(solution)/shard_map/ppermute | solution.py:247
  214.2 11.5 %up_group.6 = (f32[52,128,128]{2,1,0:T(8,128)}, bf16[52,128,128]{2,1,0:T(8,128)(2,1)}) custom-call(s32[59]{0:T(128)} %get-tuple-element.224.meta, bf16[128,6144]{1,0:T(8,128)(2,1)} %copy-done, bf16[128,6144]{1,0:T(8,128)(2,1)} %collective-permute-done.11.refs_1_, bf16[128,6144]{1,0:T(8,128)(2,1)} %collective-permute-done.12.refs_2_, ...), custom_call_target="tpu_custom_call" | custom-call | flops 201326592 | bytes 1572864 | tf_op jit(solution)/shard_map/up_group/pallas_call | solution.py:112
  225.7 4.6 collective-permute-done.23.refs_3_
  232.8 11.5 %up_group.7 = (f32[52,128,128]{2,1,0:T(8,128)}, bf16[52,128,128]{2,1,0:T(8,128)(2,1)}) custom-call(s32[59]{0:T(128)} %get-tuple-element.223.meta, bf16[128,6144]{1,0:T(8,128)(2,1)} %copy-done.1, bf16[128,6144]{1,0:T(8,128)(2,1)} %copy-done.6, bf16[128,6144]{1,0:T(8,128)(2,1)} %copy-done.7, bf16[64,6144]{1,0:T(8,128)(2,1)} %copy-done.29, ...), custom_call_target="tpu_custom_call" | custom-call | flops 201326592 | bytes 1572864 | tf_op jit(solution)/shard_map/up_group/pallas_call | solution.py:112
  245.7 15.1 %down_group.5 = (bf16[128,6144]{1,0:T(8,128)(2,1)}, bf16[128,6144]{1,0:T(8,128)(2,1)}, bf16[128,6144]{1,0:T(8,128)(2,1)}, bf16[64,6144]{1,0:T(8,128)(2,1)}, bf16[64,6144]{1,0:T(8,128)(2,1)}) custom-call(s32[59]{0:T(128)} %get-tuple-element.225.meta, f32[52,128,128]{2,1,0:T(8,128)} %get-tuple-element.141.own_ref, bf16[52,128,128]{2,1,0:T(8,128)(2,1)} %copy-done.8, ...), custom_call_target="tpu_custom_call" | custom-call | flops 201326592 | bytes 1572864 | tf_op jit(solution)/shard_map/down_group/pallas_call | solution.py:205
  266.7 14.3 %down_group.7 = (bf16[128,6144]{1,0:T(8,128)(2,1)}, bf16[128,6144]{1,0:T(8,128)(2,1)}, bf16[128,6144]{1,0:T(8,128)(2,1)}, bf16[64,6144]{1,0:T(8,128)(2,1)}, bf16[64,6144]{1,0:T(8,128)(2,1)}) custom-call(s32[59]{0:T(128)} %get-tuple-element.223.meta, f32[52,128,128]{2,1,0:T(8,128)} %get-tuple-element.165.own_ref, bf16[52,128,128]{2,1,0:T(8,128)(2,1)} %copy-done.11, ...), custom_call_target="tpu_custom_call" | custom-call | flops 201326592 | bytes 1572864 | tf_op jit(solution)/shard_map/down_group/pallas_call | solution.py:205
  282.2 14.9 %down_group.6 = (bf16[128,6144]{1,0:T(8,128)(2,1)}, bf16[128,6144]{1,0:T(8,128)(2,1)}, bf16[128,6144]{1,0:T(8,128)(2,1)}, bf16[64,6144]{1,0:T(8,128)(2,1)}, bf16[64,6144]{1,0:T(8,128)(2,1)}) custom-call(s32[59]{0:T(128)} %get-tuple-element.224.meta, f32[52,128,128]{2,1,0:T(8,128)} %get-tuple-element.158.own_ref, bf16[52,128,128]{2,1,0:T(8,128)(2,1)} %copy-done.10, ...), custom_call_target="tpu_custom_call" | custom-call | flops 201326592 | bytes 1572864 | tf_op jit(solution)/shard_map/down_group/pallas_call | solution.py:205
  301.3 16.3 %collective-permute-done.29.x_add = bf16[64,6144]{1,0:T(8,128)(2,1)S(1)} collective-permute-done((bf16[64,6144]{1,0:T(8,128)(2,1)S(1)}, bf16[64,6144]{1,0:T(8,128)(2,1)S(1)}, u32[]{:S(2)}, u32[]{:S(2)}) %collective-permute-start.29) | collective-permute-done | bytes 786464 | tf_op jit(solution)/shard_map/ppermute | solution.py:247
  323.2 10.5 %collective-permute-done.31.x_add = bf16[64,6144]{1,0:T(8,128)(2,1)S(1)} collective-permute-done((bf16[64,6144]{1,0:T(8,128)(2,1)}, bf16[64,6144]{1,0:T(8,128)(2,1)S(1)}, u32[]{:S(2)}, u32[]{:S(2)}) %collective-permute-start.31) | collective-permute-done | bytes 786464 | tf_op jit(solution)/shard_map/ppermute | solution.py:247
  342.7 29.7 %collective-permute-done.35 = bf16[128,6144]{1,0:T(8,128)(2,1)S(1)} collective-permute-done((bf16[128,6144]{1,0:T(8,128)(2,1)}, bf16[128,6144]{1,0:T(8,128)(2,1)S(1)}, u32[]{:S(2)}, u32[]{:S(2)}) %collective-permute-start.35) | collective-permute-done | bytes 1572896 | tf_op jit(solution)/shard_map/ppermute | solution.py:247
  376.2 6.2 %collective-permute-start.39 = (bf16[128,6144]{1,0:T(8,128)(2,1)S(1)}, bf16[128,6144]{1,0:T(8,128)(2,1)}, u32[]{:S(2)}, u32[]{:S(2)}) collective-permute-start(bf16[128,6144]{1,0:T(8,128)(2,1)S(1)} %add_convert_fusion.5), channel_id=1, source_target_pairs={{0,8},{2,10},{4,12},{6,14},{24,16},{26,18},{28,20},{30,22},{1,9},{... | collective-permute-start | bytes 4718600 | tf_op jit(solution)/shard_map/ppermute | solution.py:285
  386.1 3.9 add_diagonal.6
  389.9 14.6 %collective-permute-done.33 = bf16[128,6144]{1,0:T(8,128)(2,1)} collective-permute-done((bf16[128,6144]{1,0:T(8,128)(2,1)}, bf16[128,6144]{1,0:T(8,128)(2,1)}, u32[]{:S(2)}, u32[]{:S(2)}) %collective-permute-start.33) | collective-permute-done | bytes 1572896 | tf_op jit(solution)/shard_map/ppermute | solution.py:247
  407.7 5.7 %collective-permute-start.44 = (bf16[128,6144]{1,0:T(8,128)(2,1)S(1)}, bf16[128,6144]{1,0:T(8,128)(2,1)S(1)}, u32[]{:S(2)}, u32[]{:S(2)}) collective-permute-start(bf16[128,6144]{1,0:T(8,128)(2,1)S(1)} %add_convert_fusion.2), channel_id=1, source_target_pairs={{0,8},{2,10},{4,12},{6,14},{24,16},{26,18},{28,20},{30,22},{1,9},{... | collective-permute-start | bytes 4718600 | tf_op jit(solution)/shard_map/ppermute | solution.py:285
  419.5 25.9 %collective-permute-done.44 = bf16[128,6144]{1,0:T(8,128)(2,1)S(1)} collective-permute-done((bf16[128,6144]{1,0:T(8,128)(2,1)S(1)}, bf16[128,6144]{1,0:T(8,128)(2,1)S(1)}, u32[]{:S(2)}, u32[]{:S(2)}) %collective-permute-start.44) | collective-permute-done | bytes 1572896 | tf_op jit(solution)/shard_map/ppermute | solution.py:285
  446.7 4.2 collective-permute-done.41
  455.0 26.3 %collective-permute-done.37 = bf16[128,6144]{1,0:T(8,128)(2,1)S(1)} collective-permute-done((bf16[128,6144]{1,0:T(8,128)(2,1)S(1)}, bf16[128,6144]{1,0:T(8,128)(2,1)S(1)}, u32[]{:S(2)}, u32[]{:S(2)}) %collective-permute-start.37) | collective-permute-done | bytes 1572896 | tf_op jit(solution)/shard_map/ppermute | solution.py:247
  (199 shorter events, 107.3 us)
Async XLA Ops:
  0.0 37.7 %collective-permute-start = (bf16[128,6144]{1,0:T(8,128)(2,1)}, bf16[128,6144]{1,0:T(8,128)(2,1)}, u32[]{:S(2)}, u32[]{:S(2)}) collective-permute-start(bf16[128,6144]{1,0:T(8,128)(2,1)} %refs_0_.1), channel_id=1, source_target_pairs={{0,8},{2,10},{4,12},{6,14},{8,0},{10,2},{12,4},{14,6},{16,24},{18,... | collective-permute-start | bytes 4718600 | tf_op jit(solution)/shard_map/ppermute | solution.py:247
  44.7 53.3 %collective-permute-start.4 = (bf16[128,6144]{1,0:T(8,128)(2,1)}, bf16[128,6144]{1,0:T(8,128)(2,1)}, u32[]{:S(2)}, u32[]{:S(2)}) collective-permute-start(bf16[128,6144]{1,0:T(8,128)(2,1)} %collective-permute-done.refs_0_), channel_id=1, source_target_pairs={{8,16},{10,18},{12,20},{14,22},{16,8},{18,10},{20,12},{22,14},{9,1... | collective-permute-start | bytes 4718600 | tf_op jit(solution)/shard_map/ppermute | solution.py:285
  46.5 51.4 %collective-permute-start.6 = (bf16[128,6144]{1,0:T(8,128)(2,1)}, bf16[128,6144]{1,0:T(8,128)(2,1)S(1)}, u32[]{:S(2)}, u32[]{:S(2)}) collective-permute-start(bf16[128,6144]{1,0:T(8,128)(2,1)} %collective-permute-done.refs_0_), channel_id=1, source_target_pairs={{0,2},{2,0},{4,6},{6,4},{8,10},{10,8},{12,14},{14,12},{16,18},{18,... | collective-permute-start | bytes 4718600 | tf_op jit(solution)/shard_map/ppermute | solution.py:247
  47.2 50.8 %collective-permute-start.7 = (bf16[128,6144]{1,0:T(8,128)(2,1)}, bf16[128,6144]{1,0:T(8,128)(2,1)S(1)}, u32[]{:S(2)}, u32[]{:S(2)}) collective-permute-start(bf16[128,6144]{1,0:T(8,128)(2,1)} %collective-permute-done.refs_0_), channel_id=1, source_target_pairs={{0,4},{2,6},{4,0},{6,2},{8,12},{10,14},{12,8},{14,10},{16,20},{18,... | collective-permute-start | bytes 4718600 | tf_op jit(solution)/shard_map/ppermute | solution.py:247
  47.7 52.4 %collective-permute-start.5 = (bf16[128,6144]{1,0:T(8,128)(2,1)}, bf16[128,6144]{1,0:T(8,128)(2,1)}, u32[]{:S(2)}, u32[]{:S(2)}) collective-permute-start(bf16[128,6144]{1,0:T(8,128)(2,1)} %collective-permute-done.1), channel_id=1, source_target_pairs={{8,0},{10,2},{12,4},{14,6},{16,24},{18,26},{20,28},{22,30},{9,1},{... | collective-permute-start | bytes 4718600 | tf_op jit(solution)/shard_map/ppermute | solution.py:285
  101.6 50.7 %collective-permute-start.11 = (bf16[128,6144]{1,0:T(8,128)(2,1)S(1)}, bf16[128,6144]{1,0:T(8,128)(2,1)}, u32[]{:S(2)}, u32[]{:S(2)}) collective-permute-start(bf16[128,6144]{1,0:T(8,128)(2,1)S(1)} %broadcast_select_fusion.1.refs_0_), channel_id=1, source_target_pairs={{0,2},{2,0},{4,6},{6,4},{8,10},{10,8},{12,14},{14,12},{16,18},{18,... | collective-permute-start | bytes 4718600 | tf_op jit(solution)/shard_map/ppermute | solution.py:247
  102.3 50.0 %collective-permute-start.12 = (bf16[128,6144]{1,0:T(8,128)(2,1)S(1)}, bf16[128,6144]{1,0:T(8,128)(2,1)}, u32[]{:S(2)}, u32[]{:S(2)}) collective-permute-start(bf16[128,6144]{1,0:T(8,128)(2,1)S(1)} %broadcast_select_fusion.1.refs_0_), channel_id=1, source_target_pairs={{0,4},{2,6},{4,0},{6,2},{8,12},{10,14},{12,8},{14,10},{16,20},{18,... | collective-permute-start | bytes 4718600 | tf_op jit(solution)/shard_map/ppermute | solution.py:247
  102.8 49.5 %collective-permute-start.10 = (bf16[128,6144]{1,0:T(8,128)(2,1)}, bf16[128,6144]{1,0:T(8,128)(2,1)}, u32[]{:S(2)}, u32[]{:S(2)}) collective-permute-start(bf16[128,6144]{1,0:T(8,128)(2,1)} %collective-permute-done.4), channel_id=1, source_target_pairs={{8,0},{10,2},{12,4},{14,6},{16,24},{18,26},{20,28},{22,30},{9,1},{... | collective-permute-start | bytes 4718600 | tf_op jit(solution)/shard_map/ppermute | solution.py:285
  106.4 46.0 %collective-permute-start.13 = (bf16[64,6144]{1,0:T(8,128)(2,1)}, bf16[64,6144]{1,0:T(8,128)(2,1)S(1)}, u32[]{:S(2)}, u32[]{:S(2)}) collective-permute-start(bf16[64,6144]{1,0:T(8,128)(2,1)} %slice.42), channel_id=1, source_target_pairs={{0,4},{2,6},{4,0},{6,2},{8,12},{10,14},{12,8},{14,10},{16,20},{18,... | collective-permute-start | bytes 2359304 | tf_op jit(solution)/shard_map/ppermute | solution.py:247
  107.9 44.4 %collective-permute-start.14 = (bf16[64,6144]{1,0:T(8,128)(2,1)S(1)}, bf16[64,6144]{1,0:T(8,128)(2,1)}, u32[]{:S(2)}, u32[]{:S(2)}) collective-permute-start(bf16[64,6144]{1,0:T(8,128)(2,1)S(1)} %slice.43), channel_id=1, source_target_pairs={{0,2},{2,0},{4,6},{6,4},{8,10},{10,8},{12,14},{14,12},{16,18},{18,... | collective-permute-start | bytes 2359304 | tf_op jit(solution)/shard_map/ppermute | solution.py:247
  154.8 54.9 %collective-permute-start.15 = (bf16[128,6144]{1,0:T(8,128)(2,1)S(1)}, bf16[128,6144]{1,0:T(8,128)(2,1)S(1)}, u32[]{:S(2)}, u32[]{:S(2)}) collective-permute-start(bf16[128,6144]{1,0:T(8,128)(2,1)S(1)} %broadcast_select_fusion.refs_0_), channel_id=1, source_target_pairs={{0,2},{2,0},{4,6},{6,4},{8,10},{10,8},{12,14},{14,12},{16,18},{18,... | collective-permute-start | bytes 4718600 | tf_op jit(solution)/shard_map/ppermute | solution.py:247
  156.3 53.5 %collective-permute-start.16 = (bf16[128,6144]{1,0:T(8,128)(2,1)S(1)}, bf16[128,6144]{1,0:T(8,128)(2,1)S(1)}, u32[]{:S(2)}, u32[]{:S(2)}) collective-permute-start(bf16[128,6144]{1,0:T(8,128)(2,1)S(1)} %broadcast_select_fusion.refs_0_), channel_id=1, source_target_pairs={{0,4},{2,6},{4,0},{6,2},{8,12},{10,14},{12,8},{14,10},{16,20},{18,... | collective-permute-start | bytes 4718600 | tf_op jit(solution)/shard_map/ppermute | solution.py:247
  158.0 51.8 %collective-permute-start.17 = (bf16[64,6144]{1,0:T(8,128)(2,1)S(1)}, bf16[64,6144]{1,0:T(8,128)(2,1)}, u32[]{:S(2)}, u32[]{:S(2)}) collective-permute-start(bf16[64,6144]{1,0:T(8,128)(2,1)S(1)} %slice.45), channel_id=1, source_target_pairs={{0,4},{2,6},{4,0},{6,2},{8,12},{10,14},{12,8},{14,10},{16,20},{18,... | collective-permute-start | bytes 2359304 | tf_op jit(solution)/shard_map/ppermute | solution.py:247
  160.7 49.0 %collective-permute-start.18 = (bf16[64,6144]{1,0:T(8,128)(2,1)S(1)}, bf16[64,6144]{1,0:T(8,128)(2,1)}, u32[]{:S(2)}, u32[]{:S(2)}) collective-permute-start(bf16[64,6144]{1,0:T(8,128)(2,1)S(1)} %slice.46), channel_id=1, source_target_pairs={{0,2},{2,0},{4,6},{6,4},{8,10},{10,8},{12,14},{14,12},{16,18},{18,... | collective-permute-start | bytes 2359304 | tf_op jit(solution)/shard_map/ppermute | solution.py:247
  212.1 48.7 %collective-permute-start.20 = (bf16[64,6144]{1,0:T(8,128)(2,1)}, bf16[64,6144]{1,0:T(8,128)(2,1)S(1)}, u32[]{:S(2)}, u32[]{:S(2)}) collective-permute-start(bf16[64,6144]{1,0:T(8,128)(2,1)} %get-tuple-element.139), channel_id=1, source_target_pairs={{0,4},{2,6},{4,0},{6,2},{8,12},{10,14},{12,8},{14,10},{16,20},{18,... | collective-permute-start | bytes 2359304 | tf_op jit(solution)/shard_map/ppermute | solution.py:247
  212.8 48.0 %collective-permute-start.21 = (bf16[64,6144]{1,0:T(8,128)(2,1)}, bf16[64,6144]{1,0:T(8,128)(2,1)S(1)}, u32[]{:S(2)}, u32[]{:S(2)}) collective-permute-start(bf16[64,6144]{1,0:T(8,128)(2,1)} %get-tuple-element.140), channel_id=1, source_target_pairs={{0,2},{2,0},{4,6},{6,4},{8,10},{10,8},{12,14},{14,12},{16,18},{18,... | collective-permute-start | bytes 2359304 | tf_op jit(solution)/shard_map/ppermute | solution.py:247
  334.9 37.5 %collective-permute-start.35 = (bf16[128,6144]{1,0:T(8,128)(2,1)}, bf16[128,6144]{1,0:T(8,128)(2,1)S(1)}, u32[]{:S(2)}, u32[]{:S(2)}) collective-permute-start(bf16[128,6144]{1,0:T(8,128)(2,1)} %get-tuple-element.198), channel_id=1, source_target_pairs={{0,2},{2,0},{4,6},{6,4},{8,10},{10,8},{12,14},{14,12},{16,18},{18,... | collective-permute-start | bytes 4718600 | tf_op jit(solution)/shard_map/ppermute | solution.py:247
  335.6 38.0 %collective-permute-start.36 = (bf16[128,6144]{1,0:T(8,128)(2,1)}, bf16[128,6144]{1,0:T(8,128)(2,1)}, u32[]{:S(2)}, u32[]{:S(2)}) collective-permute-start(bf16[128,6144]{1,0:T(8,128)(2,1)} %get-tuple-element.199), channel_id=1, source_target_pairs={{0,4},{2,6},{4,0},{6,2},{8,12},{10,14},{12,8},{14,10},{16,20},{18,... | collective-permute-start | bytes 4718600 | tf_op jit(solution)/shard_map/ppermute | solution.py:247
  340.8 63.7 %collective-permute-start.33 = (bf16[128,6144]{1,0:T(8,128)(2,1)}, bf16[128,6144]{1,0:T(8,128)(2,1)}, u32[]{:S(2)}, u32[]{:S(2)}) collective-permute-start(bf16[128,6144]{1,0:T(8,128)(2,1)} %get-tuple-element.195), channel_id=1, source_target_pairs={{0,2},{2,0},{4,6},{6,4},{8,10},{10,8},{12,14},{14,12},{16,18},{18,... | collective-permute-start | bytes 4718600 | tf_op jit(solution)/shard_map/ppermute | solution.py:247
  342.2 62.8 %collective-permute-start.34 = (bf16[128,6144]{1,0:T(8,128)(2,1)}, bf16[128,6144]{1,0:T(8,128)(2,1)}, u32[]{:S(2)}, u32[]{:S(2)}) collective-permute-start(bf16[128,6144]{1,0:T(8,128)(2,1)} %get-tuple-element.196), channel_id=1, source_target_pairs={{0,4},{2,6},{4,0},{6,2},{8,12},{10,14},{12,8},{14,10},{16,20},{18,... | collective-permute-start | bytes 4718600 | tf_op jit(solution)/shard_map/ppermute | solution.py:247
  376.2 39.5 %collective-permute-start.39 = (bf16[128,6144]{1,0:T(8,128)(2,1)S(1)}, bf16[128,6144]{1,0:T(8,128)(2,1)}, u32[]{:S(2)}, u32[]{:S(2)}) collective-permute-start(bf16[128,6144]{1,0:T(8,128)(2,1)S(1)} %add_convert_fusion.5), channel_id=1, source_target_pairs={{0,8},{2,10},{4,12},{6,14},{24,16},{26,18},{28,20},{30,22},{1,9},{... | collective-permute-start | bytes 4718600 | tf_op jit(solution)/shard_map/ppermute | solution.py:285
  407.7 37.7 %collective-permute-start.44 = (bf16[128,6144]{1,0:T(8,128)(2,1)S(1)}, bf16[128,6144]{1,0:T(8,128)(2,1)S(1)}, u32[]{:S(2)}, u32[]{:S(2)}) collective-permute-start(bf16[128,6144]{1,0:T(8,128)(2,1)S(1)} %add_convert_fusion.2), channel_id=1, source_target_pairs={{0,8},{2,10},{4,12},{6,14},{24,16},{26,18},{28,20},{30,22},{1,9},{... | collective-permute-start | bytes 4718600 | tf_op jit(solution)/shard_map/ppermute | solution.py:285
  413.5 37.4 %collective-permute-start.41 = (bf16[128,6144]{1,0:T(8,128)(2,1)S(1)}, bf16[128,6144]{1,0:T(8,128)(2,1)S(1)}, u32[]{:S(2)}, u32[]{:S(2)}) collective-permute-start(bf16[128,6144]{1,0:T(8,128)(2,1)S(1)} %copy-done.14), channel_id=1, source_target_pairs={{0,2},{2,0},{4,6},{6,4},{8,10},{10,8},{12,14},{14,12},{16,18},{18,... | collective-permute-start | bytes 4718600 | tf_op jit(solution)/shard_map/ppermute | solution.py:247
  418.4 63.0 %collective-permute-start.37 = (bf16[128,6144]{1,0:T(8,128)(2,1)S(1)}, bf16[128,6144]{1,0:T(8,128)(2,1)S(1)}, u32[]{:S(2)}, u32[]{:S(2)}) collective-permute-start(bf16[128,6144]{1,0:T(8,128)(2,1)S(1)} %copy-done.12), channel_id=1, source_target_pairs={{0,2},{2,0},{4,6},{6,4},{8,10},{10,8},{12,14},{14,12},{16,18},{18,... | collective-permute-start | bytes 4718600 | tf_op jit(solution)/shard_map/ppermute | solution.py:247
  (60 other events, 1093.7 us)

commit v3 on v2

--- a/solution.py
+++ b/solution.py
@@ -12,7 +12,7 @@
 HALF = BLK // 2
 PLANE = 4
 LAYERS = 4
-DEPTH = 3
+DEPTH = 5
 VMEM_BYTES = 56 * 1024 * 1024
 
 
@@ -169,14 +169,19 @@
         one = hidden_of(slot, 0, left)
         two = jnp.where(right < 0, 0.0, hidden_of(slot, 1, jnp.maximum(right, 0)))
         hidden = jnp.concatenate([one, two], axis=1).astype(jnp.bfloat16)
-        for at in range(0, width, piece):
-            cols = pl.ds(at, piece)
-            term = jnp.dot(hidden, held[slot, :, cols], preferred_element_type=jnp.float32)
-            total[:, cols] = jnp.where(first, 0.0, total[:, cols]) + term
-
-        @pl.when(last)
-        def _():
-            done[offset] = total[...].astype(jnp.bfloat16)
+        for is_first in (True, False):
+            for is_last in (True, False):
+                @pl.when((first == is_first) & (last == is_last))
+                def _():
+                    for at in range(0, width, piece):
+                        cols = pl.ds(at, piece)
+                        term = jnp.dot(hidden, held[slot, :, cols], preferred_element_type=jnp.float32)
+                        if not is_first:
+                            term = total[:, cols] + term
+                        if is_last:
+                            done[offset, :, cols] = term.astype(jnp.bfloat16)
+                        else:
+                            total[:, cols] = term
 
         for o in range(PLANE):
             @pl.when(last & (offset == o))
@@ -229,7 +234,7 @@
 
 def add_diagonal(over_x, over_y, x_add, y_add):
     feat = over_x.shape[1]
-    steps = 3
+    steps = 6 if feat % (6 * BLK) == 0 else 1
     upper = pl.BlockSpec((HALF, feat // steps), lambda i: (0, i))
     lower = pl.BlockSpec((HALF, feat // steps), lambda i: (1, i))
     return pl.pallas_call(

time: 488 us -> 487 us (level)
    pallas_call x4, Pallas kernels: 15.1 us -> 20 us  [add_diagonal(): pl.pallas_call(add_kernel, grid=(steps,), in_specs=[upper, lower, upper,...]
where the time goes in v3:
time: 487 us; the launch traced here: 486 us
  waiting for transfers between devices  268 us (55%)
  Pallas kernels  121 us (25%)
  starting transfers between devices  58.2 us (12%)
  local copies, waits for them, and re-layouts  20.3 us (4%)
  other arithmetic  17.3 us (4%)
    ppermute x34, waiting for transfers between devices, swap(): lax.ppermute(value, 'wa', [(w, w ^ bits) for w in range(LAYERS * PLANE)])  240 us
    pallas_call x4, Pallas kernels, down_group(): pl.pallas_call(functools.partial(down_kernel, per_owner, own.shape[0]), i...  57.1 us
    pallas_call x4, Pallas kernels, up_group(): pl.pallas_call(functools.partial(up_kernel, per_owner), in_specs=[pl.Bloc...  44.3 us
    ppermute x34, starting transfers between devices, swap(): lax.ppermute(value, 'wa', [(w, w ^ bits) for w in range(LAYERS * PLANE)])  37.5 us
    ppermute x8, waiting for transfers between devices, along_z(): return lax.ppermute(value, 'wa', pairs)  25.9 us
    ppermute x8, starting transfers between devices, along_z(): return lax.ppermute(value, 'wa', pairs)  20.2 us
    pallas_call x4, Pallas kernels, add_diagonal(): pl.pallas_call(add_kernel, grid=(steps,), in_specs=[upper, lower, upper,...  20 us
    unnamed x76, local copies, waits for them, and re-layouts  13.7 us
  transfers between devices with their start and end apart: 46, of which 22 were waited for; matrix products, arithmetic and copies ran while one was open for 4% of the time, Pallas kernels for 25%

profile of v3, /device:TPU:0, one launch (start us, length us, event | category | flops | bytes accessed | tf_op | source)
XLA Modules:
  0.0 485.6 jit_solution(15059579609005671392)
XLA Ops:
  7.9 29.9 %collective-permute-done.refs_0_ = bf16[128,6144]{1,0:T(8,128)(2,1)} collective-permute-done((bf16[128,6144]{1,0:T(8,128)(2,1)}, bf16[128,6144]{1,0:T(8,128)(2,1)}, u32[]{:S(2)}, u32[]{:S(2)}) %collective-permute-start) | collective-permute-done | bytes 1572896 | tf_op jit(solution)/shard_map/ppermute | solution.py:252
  50.3 13.7 %collective-permute-done.8.refs_3_ = bf16[64,6144]{1,0:T(8,128)(2,1)} collective-permute-done((bf16[64,6144]{1,0:T(8,128)(2,1)}, bf16[64,6144]{1,0:T(8,128)(2,1)}, u32[]{:S(2)}, u32[]{:S(2)}) %collective-permute-start.8) | collective-permute-done | bytes 786464 | tf_op jit(solution)/shard_map/ppermute | solution.py:252
  65.4 32.5 %collective-permute-done.9.refs_4_ = bf16[64,6144]{1,0:T(8,128)(2,1)S(1)} collective-permute-done((bf16[64,6144]{1,0:T(8,128)(2,1)S(1)}, bf16[64,6144]{1,0:T(8,128)(2,1)S(1)}, u32[]{:S(2)}, u32[]{:S(2)}) %collective-permute-start.9) | collective-permute-done | bytes 786464 | tf_op jit(solution)/shard_map/ppermute | solution.py:252
  111.4 11.1 %up_group.4 = (f32[52,128,128]{2,1,0:T(8,128)}, bf16[52,128,128]{2,1,0:T(8,128)(2,1)}) custom-call(s32[59]{0:T(128)} %get-tuple-element.226.meta, bf16[128,6144]{1,0:T(8,128)(2,1)} %refs_0_.1, bf16[128,6144]{1,0:T(8,128)(2,1)} %copy-done.5, bf16[128,6144]{1,0:T(8,128)(2,1)} %collective-permute-done.3.refs_2_, ...), custom_call_target="tpu_custom_call" | custom-call | flops 201326592 | bytes 1572864 | tf_op jit(solution)/shard_map/up_group/pallas_call | solution.py:112
  122.5 29.9 %collective-permute-done.13.refs_3_ = bf16[64,6144]{1,0:T(8,128)(2,1)S(1)} collective-permute-done((bf16[64,6144]{1,0:T(8,128)(2,1)}, bf16[64,6144]{1,0:T(8,128)(2,1)S(1)}, u32[]{:S(2)}, u32[]{:S(2)}) %collective-permute-start.13) | collective-permute-done | bytes 786464 | tf_op jit(solution)/shard_map/ppermute | solution.py:252
  161.5 11.1 %up_group.5 = (f32[52,128,128]{2,1,0:T(8,128)}, bf16[52,128,128]{2,1,0:T(8,128)(2,1)}) custom-call(s32[59]{0:T(128)} %get-tuple-element.225.meta, bf16[128,6144]{1,0:T(8,128)(2,1)} %collective-permute-done.refs_0_, bf16[128,6144]{1,0:T(8,128)(2,1)} %copy-done.2, bf16[128,6144]{1,0:T(8,128)(2,1)} %copy-done.3, bf16[64,6144]{1,0:T(8,128)(2,1)} %copy-done.28, ...), custom_call_target="tpu_custom_call" | custom-call | flops 201326592 | bytes 1572864 | tf_op jit(solution)/shard_map/up_group/pallas_call | solution.py:112
  173.9 14.5 %down_group.4 = (bf16[128,6144]{1,0:T(8,128)(2,1)}, bf16[128,6144]{1,0:T(8,128)(2,1)}, bf16[128,6144]{1,0:T(8,128)(2,1)}, bf16[64,6144]{1,0:T(8,128)(2,1)}, bf16[64,6144]{1,0:T(8,128)(2,1)}) custom-call(s32[59]{0:T(128)} %get-tuple-element.226.meta, f32[52,128,128]{2,1,0:T(8,128)} %get-tuple-element.128.own_ref, bf16[52,128,128]{2,1,0:T(8,128)(2,1)} %copy-done.9, ...), custom_call_target="tpu_custom_call" | custom-call | flops 201326592 | bytes 1572864 | tf_op jit(solution)/shard_map/down_group/pallas_call | solution.py:210
  188.4 21.4 %collective-permute-done.17.refs_3_ = bf16[64,6144]{1,0:T(8,128)(2,1)} collective-permute-done((bf16[64,6144]{1,0:T(8,128)(2,1)S(1)}, bf16[64,6144]{1,0:T(8,128)(2,1)}, u32[]{:S(2)}, u32[]{:S(2)}) %collective-permute-start.17) | collective-permute-done | bytes 786464 | tf_op jit(solution)/shard_map/ppermute | solution.py:252
  214.2 11.1 %up_group.6 = (f32[52,128,128]{2,1,0:T(8,128)}, bf16[52,128,128]{2,1,0:T(8,128)(2,1)}) custom-call(s32[59]{0:T(128)} %get-tuple-element.224.meta, bf16[128,6144]{1,0:T(8,128)(2,1)} %copy-done, bf16[128,6144]{1,0:T(8,128)(2,1)} %collective-permute-done.11.refs_1_, bf16[128,6144]{1,0:T(8,128)(2,1)} %collective-permute-done.12.refs_2_, ...), custom_call_target="tpu_custom_call" | custom-call | flops 201326592 | bytes 1572864 | tf_op jit(solution)/shard_map/up_group/pallas_call | solution.py:112
  225.2 5.1 %collective-permute-done.23.refs_3_ = bf16[64,6144]{1,0:T(8,128)(2,1)S(1)} collective-permute-done((bf16[64,6144]{1,0:T(8,128)(2,1)S(1)}, bf16[64,6144]{1,0:T(8,128)(2,1)S(1)}, u32[]{:S(2)}, u32[]{:S(2)}) %collective-permute-start.23) | collective-permute-done | bytes 786464 | tf_op jit(solution)/shard_map/ppermute | solution.py:252
  232.8 11.1 %up_group.7 = (f32[52,128,128]{2,1,0:T(8,128)}, bf16[52,128,128]{2,1,0:T(8,128)(2,1)}) custom-call(s32[59]{0:T(128)} %get-tuple-element.223.meta, bf16[128,6144]{1,0:T(8,128)(2,1)} %copy-done.1, bf16[128,6144]{1,0:T(8,128)(2,1)} %copy-done.6, bf16[128,6144]{1,0:T(8,128)(2,1)} %copy-done.7, bf16[64,6144]{1,0:T(8,128)(2,1)} %copy-done.29, ...), custom_call_target="tpu_custom_call" | custom-call | flops 201326592 | bytes 1572864 | tf_op jit(solution)/shard_map/up_group/pallas_call | solution.py:112
  245.2 14.2 %down_group.5 = (bf16[128,6144]{1,0:T(8,128)(2,1)}, bf16[128,6144]{1,0:T(8,128)(2,1)}, bf16[128,6144]{1,0:T(8,128)(2,1)}, bf16[64,6144]{1,0:T(8,128)(2,1)}, bf16[64,6144]{1,0:T(8,128)(2,1)}) custom-call(s32[59]{0:T(128)} %get-tuple-element.225.meta, f32[52,128,128]{2,1,0:T(8,128)} %get-tuple-element.141.own_ref, bf16[52,128,128]{2,1,0:T(8,128)(2,1)} %copy-done.8, ...), custom_call_target="tpu_custom_call" | custom-call | flops 201326592 | bytes 1572864 | tf_op jit(solution)/shard_map/down_group/pallas_call | solution.py:210
  265.4 14.4 %down_group.7 = (bf16[128,6144]{1,0:T(8,128)(2,1)}, bf16[128,6144]{1,0:T(8,128)(2,1)}, bf16[128,6144]{1,0:T(8,128)(2,1)}, bf16[64,6144]{1,0:T(8,128)(2,1)}, bf16[64,6144]{1,0:T(8,128)(2,1)}) custom-call(s32[59]{0:T(128)} %get-tuple-element.223.meta, f32[52,128,128]{2,1,0:T(8,128)} %get-tuple-element.165.own_ref, bf16[52,128,128]{2,1,0:T(8,128)(2,1)} %copy-done.11, ...), custom_call_target="tpu_custom_call" | custom-call | flops 201326592 | bytes 1572864 | tf_op jit(solution)/shard_map/down_group/pallas_call | solution.py:210
  281.1 14.0 %down_group.6 = (bf16[128,6144]{1,0:T(8,128)(2,1)}, bf16[128,6144]{1,0:T(8,128)(2,1)}, bf16[128,6144]{1,0:T(8,128)(2,1)}, bf16[64,6144]{1,0:T(8,128)(2,1)}, bf16[64,6144]{1,0:T(8,128)(2,1)}) custom-call(s32[59]{0:T(128)} %get-tuple-element.224.meta, f32[52,128,128]{2,1,0:T(8,128)} %get-tuple-element.158.own_ref, bf16[52,128,128]{2,1,0:T(8,128)(2,1)} %copy-done.10, ...), custom_call_target="tpu_custom_call" | custom-call | flops 201326592 | bytes 1572864 | tf_op jit(solution)/shard_map/down_group/pallas_call | solution.py:210
  299.2 16.3 %collective-permute-done.29.x_add = bf16[64,6144]{1,0:T(8,128)(2,1)S(1)} collective-permute-done((bf16[64,6144]{1,0:T(8,128)(2,1)S(1)}, bf16[64,6144]{1,0:T(8,128)(2,1)S(1)}, u32[]{:S(2)}, u32[]{:S(2)}) %collective-permute-start.29) | collective-permute-done | bytes 786464 | tf_op jit(solution)/shard_map/ppermute | solution.py:252
  322.3 9.3 %collective-permute-done.31.x_add = bf16[64,6144]{1,0:T(8,128)(2,1)S(1)} collective-permute-done((bf16[64,6144]{1,0:T(8,128)(2,1)}, bf16[64,6144]{1,0:T(8,128)(2,1)S(1)}, u32[]{:S(2)}, u32[]{:S(2)}) %collective-permute-start.31) | collective-permute-done | bytes 786464 | tf_op jit(solution)/shard_map/ppermute | solution.py:252
  342.1 28.5 %collective-permute-done.35 = bf16[128,6144]{1,0:T(8,128)(2,1)S(1)} collective-permute-done((bf16[128,6144]{1,0:T(8,128)(2,1)}, bf16[128,6144]{1,0:T(8,128)(2,1)S(1)}, u32[]{:S(2)}, u32[]{:S(2)}) %collective-permute-start.35) | collective-permute-done | bytes 1572896 | tf_op jit(solution)/shard_map/ppermute | solution.py:252
  374.4 6.3 %collective-permute-start.39 = (bf16[128,6144]{1,0:T(8,128)(2,1)S(1)}, bf16[128,6144]{1,0:T(8,128)(2,1)}, u32[]{:S(2)}, u32[]{:S(2)}) collective-permute-start(bf16[128,6144]{1,0:T(8,128)(2,1)S(1)} %add_convert_fusion.5), channel_id=1, source_target_pairs={{0,8},{2,10},{4,12},{6,14},{24,16},{26,18},{28,20},{30,22},{1,9},{... | collective-permute-start | bytes 4718600 | tf_op jit(solution)/shard_map/ppermute | solution.py:290
  380.7 5.0 %add_diagonal.7 = (bf16[128,6144]{1,0:T(8,128)(2,1)}, bf16[128,6144]{1,0:T(8,128)(2,1)}) custom-call(bf16[128,6144]{1,0:T(8,128)(2,1)} %get-tuple-element.206.x_ref, bf16[128,6144]{1,0:T(8,128)(2,1)} %get-tuple-element.207.y_ref, bf16[64,6144]{1,0:T(8,128)(2,1)} %copy-done.21, bf16[64,6144]{1,0:T(8,128)(2,1)} %copy-done.22), custom_call_target="tpu_custom_call", output_to_operand_aliasing={{0}: (0, {}), {1}: (1, {})} | custom-call | tf_op jit(solution)/shard_map/add_diagonal/pallas_call | solution.py:240
  385.7 5.1 %add_diagonal.6 = (bf16[128,6144]{1,0:T(8,128)(2,1)}, bf16[128,6144]{1,0:T(8,128)(2,1)}) custom-call(bf16[128,6144]{1,0:T(8,128)(2,1)} %get-tuple-element.200.x_ref, bf16[128,6144]{1,0:T(8,128)(2,1)} %get-tuple-element.201.y_ref, bf16[64,6144]{1,0:T(8,128)(2,1)} %collective-permute-done.25.x_add, ...), custom_call_target="tpu_custom_call", output_to_operand_aliasing={{0}: (0, {}), {1}: (1, {})} | custom-call | tf_op jit(solution)/shard_map/add_diagonal/pallas_call | solution.py:240
  390.7 11.6 %collective-permute-done.33 = bf16[128,6144]{1,0:T(8,128)(2,1)} collective-permute-done((bf16[128,6144]{1,0:T(8,128)(2,1)}, bf16[128,6144]{1,0:T(8,128)(2,1)}, u32[]{:S(2)}, u32[]{:S(2)}) %collective-permute-start.33) | collective-permute-done | bytes 1572896 | tf_op jit(solution)/shard_map/ppermute | solution.py:252
  405.5 6.0 %collective-permute-start.44 = (bf16[128,6144]{1,0:T(8,128)(2,1)S(1)}, bf16[128,6144]{1,0:T(8,128)(2,1)S(1)}, u32[]{:S(2)}, u32[]{:S(2)}) collective-permute-start(bf16[128,6144]{1,0:T(8,128)(2,1)S(1)} %add_convert_fusion.2), channel_id=1, source_target_pairs={{0,8},{2,10},{4,12},{6,14},{24,16},{26,18},{28,20},{30,22},{1,9},{... | collective-permute-start | bytes 4718600 | tf_op jit(solution)/shard_map/ppermute | solution.py:290
  417.6 25.9 %collective-permute-done.44 = bf16[128,6144]{1,0:T(8,128)(2,1)S(1)} collective-permute-done((bf16[128,6144]{1,0:T(8,128)(2,1)S(1)}, bf16[128,6144]{1,0:T(8,128)(2,1)S(1)}, u32[]{:S(2)}, u32[]{:S(2)}) %collective-permute-start.44) | collective-permute-done | bytes 1572896 | tf_op jit(solution)/shard_map/ppermute | solution.py:290
  453.4 26.1 %collective-permute-done.37 = bf16[128,6144]{1,0:T(8,128)(2,1)S(1)} collective-permute-done((bf16[128,6144]{1,0:T(8,128)(2,1)S(1)}, bf16[128,6144]{1,0:T(8,128)(2,1)S(1)}, u32[]{:S(2)}, u32[]{:S(2)}) %collective-permute-start.37) | collective-permute-done | bytes 1572896 | tf_op jit(solution)/shard_map/ppermute | solution.py:252
  (199 shorter events, 110.9 us)
Async XLA Ops:
  0.0 37.7 %collective-permute-start = (bf16[128,6144]{1,0:T(8,128)(2,1)}, bf16[128,6144]{1,0:T(8,128)(2,1)}, u32[]{:S(2)}, u32[]{:S(2)}) collective-permute-start(bf16[128,6144]{1,0:T(8,128)(2,1)} %refs_0_.1), channel_id=1, source_target_pairs={{0,8},{2,10},{4,12},{6,14},{8,0},{10,2},{12,4},{14,6},{16,24},{18,... | collective-permute-start | bytes 4718600 | tf_op jit(solution)/shard_map/ppermute | solution.py:252
  44.7 53.3 %collective-permute-start.4 = (bf16[128,6144]{1,0:T(8,128)(2,1)}, bf16[128,6144]{1,0:T(8,128)(2,1)}, u32[]{:S(2)}, u32[]{:S(2)}) collective-permute-start(bf16[128,6144]{1,0:T(8,128)(2,1)} %collective-permute-done.refs_0_), channel_id=1, source_target_pairs={{8,16},{10,18},{12,20},{14,22},{16,8},{18,10},{20,12},{22,14},{9,1... | collective-permute-start | bytes 4718600 | tf_op jit(solution)/shard_map/ppermute | solution.py:290
  46.5 51.4 %collective-permute-start.6 = (bf16[128,6144]{1,0:T(8,128)(2,1)}, bf16[128,6144]{1,0:T(8,128)(2,1)S(1)}, u32[]{:S(2)}, u32[]{:S(2)}) collective-permute-start(bf16[128,6144]{1,0:T(8,128)(2,1)} %collective-permute-done.refs_0_), channel_id=1, source_target_pairs={{0,2},{2,0},{4,6},{6,4},{8,10},{10,8},{12,14},{14,12},{16,18},{18,... | collective-permute-start | bytes 4718600 | tf_op jit(solution)/shard_map/ppermute | solution.py:252
  47.2 50.8 %collective-permute-start.7 = (bf16[128,6144]{1,0:T(8,128)(2,1)}, bf16[128,6144]{1,0:T(8,128)(2,1)S(1)}, u32[]{:S(2)}, u32[]{:S(2)}) collective-permute-start(bf16[128,6144]{1,0:T(8,128)(2,1)} %collective-permute-done.refs_0_), channel_id=1, source_target_pairs={{0,4},{2,6},{4,0},{6,2},{8,12},{10,14},{12,8},{14,10},{16,20},{18,... | collective-permute-start | bytes 4718600 | tf_op jit(solution)/shard_map/ppermute | solution.py:252
  47.7 52.4 %collective-permute-start.5 = (bf16[128,6144]{1,0:T(8,128)(2,1)}, bf16[128,6144]{1,0:T(8,128)(2,1)}, u32[]{:S(2)}, u32[]{:S(2)}) collective-permute-start(bf16[128,6144]{1,0:T(8,128)(2,1)} %collective-permute-done.1), channel_id=1, source_target_pairs={{8,0},{10,2},{12,4},{14,6},{16,24},{18,26},{20,28},{22,30},{9,1},{... | collective-permute-start | bytes 4718600 | tf_op jit(solution)/shard_map/ppermute | solution.py:290
  101.6 50.7 %collective-permute-start.11 = (bf16[128,6144]{1,0:T(8,128)(2,1)S(1)}, bf16[128,6144]{1,0:T(8,128)(2,1)}, u32[]{:S(2)}, u32[]{:S(2)}) collective-permute-start(bf16[128,6144]{1,0:T(8,128)(2,1)S(1)} %broadcast_select_fusion.1.refs_0_), channel_id=1, source_target_pairs={{0,2},{2,0},{4,6},{6,4},{8,10},{10,8},{12,14},{14,12},{16,18},{18,... | collective-permute-start | bytes 4718600 | tf_op jit(solution)/shard_map/ppermute | solution.py:252
  102.3 50.0 %collective-permute-start.12 = (bf16[128,6144]{1,0:T(8,128)(2,1)S(1)}, bf16[128,6144]{1,0:T(8,128)(2,1)}, u32[]{:S(2)}, u32[]{:S(2)}) collective-permute-start(bf16[128,6144]{1,0:T(8,128)(2,1)S(1)} %broadcast_select_fusion.1.refs_0_), channel_id=1, source_target_pairs={{0,4},{2,6},{4,0},{6,2},{8,12},{10,14},{12,8},{14,10},{16,20},{18,... | collective-permute-start | bytes 4718600 | tf_op jit(solution)/shard_map/ppermute | solution.py:252
  102.8 49.5 %collective-permute-start.10 = (bf16[128,6144]{1,0:T(8,128)(2,1)}, bf16[128,6144]{1,0:T(8,128)(2,1)}, u32[]{:S(2)}, u32[]{:S(2)}) collective-permute-start(bf16[128,6144]{1,0:T(8,128)(2,1)} %collective-permute-done.4), channel_id=1, source_target_pairs={{8,0},{10,2},{12,4},{14,6},{16,24},{18,26},{20,28},{22,30},{9,1},{... | collective-permute-start | bytes 4718600 | tf_op jit(solution)/shard_map/ppermute | solution.py:290
  106.4 46.0 %collective-permute-start.13 = (bf16[64,6144]{1,0:T(8,128)(2,1)}, bf16[64,6144]{1,0:T(8,128)(2,1)S(1)}, u32[]{:S(2)}, u32[]{:S(2)}) collective-permute-start(bf16[64,6144]{1,0:T(8,128)(2,1)} %slice.42), channel_id=1, source_target_pairs={{0,4},{2,6},{4,0},{6,2},{8,12},{10,14},{12,8},{14,10},{16,20},{18,... | collective-permute-start | bytes 2359304 | tf_op jit(solution)/shard_map/ppermute | solution.py:252
  107.9 44.4 %collective-permute-start.14 = (bf16[64,6144]{1,0:T(8,128)(2,1)S(1)}, bf16[64,6144]{1,0:T(8,128)(2,1)}, u32[]{:S(2)}, u32[]{:S(2)}) collective-permute-start(bf16[64,6144]{1,0:T(8,128)(2,1)S(1)} %slice.43), channel_id=1, source_target_pairs={{0,2},{2,0},{4,6},{6,4},{8,10},{10,8},{12,14},{14,12},{16,18},{18,... | collective-permute-start | bytes 2359304 | tf_op jit(solution)/shard_map/ppermute | solution.py:252
  154.8 54.9 %collective-permute-start.15 = (bf16[128,6144]{1,0:T(8,128)(2,1)S(1)}, bf16[128,6144]{1,0:T(8,128)(2,1)S(1)}, u32[]{:S(2)}, u32[]{:S(2)}) collective-permute-start(bf16[128,6144]{1,0:T(8,128)(2,1)S(1)} %broadcast_select_fusion.refs_0_), channel_id=1, source_target_pairs={{0,2},{2,0},{4,6},{6,4},{8,10},{10,8},{12,14},{14,12},{16,18},{18,... | collective-permute-start | bytes 4718600 | tf_op jit(solution)/shard_map/ppermute | solution.py:252
  156.3 53.5 %collective-permute-start.16 = (bf16[128,6144]{1,0:T(8,128)(2,1)S(1)}, bf16[128,6144]{1,0:T(8,128)(2,1)S(1)}, u32[]{:S(2)}, u32[]{:S(2)}) collective-permute-start(bf16[128,6144]{1,0:T(8,128)(2,1)S(1)} %broadcast_select_fusion.refs_0_), channel_id=1, source_target_pairs={{0,4},{2,6},{4,0},{6,2},{8,12},{10,14},{12,8},{14,10},{16,20},{18,... | collective-permute-start | bytes 4718600 | tf_op jit(solution)/shard_map/ppermute | solution.py:252
  158.0 51.8 %collective-permute-start.17 = (bf16[64,6144]{1,0:T(8,128)(2,1)S(1)}, bf16[64,6144]{1,0:T(8,128)(2,1)}, u32[]{:S(2)}, u32[]{:S(2)}) collective-permute-start(bf16[64,6144]{1,0:T(8,128)(2,1)S(1)} %slice.45), channel_id=1, source_target_pairs={{0,4},{2,6},{4,0},{6,2},{8,12},{10,14},{12,8},{14,10},{16,20},{18,... | collective-permute-start | bytes 2359304 | tf_op jit(solution)/shard_map/ppermute | solution.py:252
  160.7 49.0 %collective-permute-start.18 = (bf16[64,6144]{1,0:T(8,128)(2,1)S(1)}, bf16[64,6144]{1,0:T(8,128)(2,1)}, u32[]{:S(2)}, u32[]{:S(2)}) collective-permute-start(bf16[64,6144]{1,0:T(8,128)(2,1)S(1)} %slice.46), channel_id=1, source_target_pairs={{0,2},{2,0},{4,6},{6,4},{8,10},{10,8},{12,14},{14,12},{16,18},{18,... | collective-permute-start | bytes 2359304 | tf_op jit(solution)/shard_map/ppermute | solution.py:252
  212.1 47.3 %collective-permute-start.20 = (bf16[64,6144]{1,0:T(8,128)(2,1)}, bf16[64,6144]{1,0:T(8,128)(2,1)S(1)}, u32[]{:S(2)}, u32[]{:S(2)}) collective-permute-start(bf16[64,6144]{1,0:T(8,128)(2,1)} %get-tuple-element.139), channel_id=1, source_target_pairs={{0,4},{2,6},{4,0},{6,2},{8,12},{10,14},{12,8},{14,10},{16,20},{18,... | collective-permute-start | bytes 2359304 | tf_op jit(solution)/shard_map/ppermute | solution.py:252
  212.8 46.7 %collective-permute-start.21 = (bf16[64,6144]{1,0:T(8,128)(2,1)}, bf16[64,6144]{1,0:T(8,128)(2,1)S(1)}, u32[]{:S(2)}, u32[]{:S(2)}) collective-permute-start(bf16[64,6144]{1,0:T(8,128)(2,1)} %get-tuple-element.140), channel_id=1, source_target_pairs={{0,2},{2,0},{4,6},{6,4},{8,10},{10,8},{12,14},{14,12},{16,18},{18,... | collective-permute-start | bytes 2359304 | tf_op jit(solution)/shard_map/ppermute | solution.py:252
  333.1 37.5 %collective-permute-start.35 = (bf16[128,6144]{1,0:T(8,128)(2,1)}, bf16[128,6144]{1,0:T(8,128)(2,1)S(1)}, u32[]{:S(2)}, u32[]{:S(2)}) collective-permute-start(bf16[128,6144]{1,0:T(8,128)(2,1)} %get-tuple-element.198), channel_id=1, source_target_pairs={{0,2},{2,0},{4,6},{6,4},{8,10},{10,8},{12,14},{14,12},{16,18},{18,... | collective-permute-start | bytes 4718600 | tf_op jit(solution)/shard_map/ppermute | solution.py:252
  333.7 38.1 %collective-permute-start.36 = (bf16[128,6144]{1,0:T(8,128)(2,1)}, bf16[128,6144]{1,0:T(8,128)(2,1)}, u32[]{:S(2)}, u32[]{:S(2)}) collective-permute-start(bf16[128,6144]{1,0:T(8,128)(2,1)} %get-tuple-element.199), channel_id=1, source_target_pairs={{0,4},{2,6},{4,0},{6,2},{8,12},{10,14},{12,8},{14,10},{16,20},{18,... | collective-permute-start | bytes 4718600 | tf_op jit(solution)/shard_map/ppermute | solution.py:252
  339.8 62.6 %collective-permute-start.33 = (bf16[128,6144]{1,0:T(8,128)(2,1)}, bf16[128,6144]{1,0:T(8,128)(2,1)}, u32[]{:S(2)}, u32[]{:S(2)}) collective-permute-start(bf16[128,6144]{1,0:T(8,128)(2,1)} %get-tuple-element.195), channel_id=1, source_target_pairs={{0,2},{2,0},{4,6},{6,4},{8,10},{10,8},{12,14},{14,12},{16,18},{18,... | collective-permute-start | bytes 4718600 | tf_op jit(solution)/shard_map/ppermute | solution.py:252
  341.2 61.5 %collective-permute-start.34 = (bf16[128,6144]{1,0:T(8,128)(2,1)}, bf16[128,6144]{1,0:T(8,128)(2,1)}, u32[]{:S(2)}, u32[]{:S(2)}) collective-permute-start(bf16[128,6144]{1,0:T(8,128)(2,1)} %get-tuple-element.196), channel_id=1, source_target_pairs={{0,4},{2,6},{4,0},{6,2},{8,12},{10,14},{12,8},{14,10},{16,20},{18,... | collective-permute-start | bytes 4718600 | tf_op jit(solution)/shard_map/ppermute | solution.py:252
  374.4 39.7 %collective-permute-start.39 = (bf16[128,6144]{1,0:T(8,128)(2,1)S(1)}, bf16[128,6144]{1,0:T(8,128)(2,1)}, u32[]{:S(2)}, u32[]{:S(2)}) collective-permute-start(bf16[128,6144]{1,0:T(8,128)(2,1)S(1)} %add_convert_fusion.5), channel_id=1, source_target_pairs={{0,8},{2,10},{4,12},{6,14},{24,16},{26,18},{28,20},{30,22},{1,9},{... | collective-permute-start | bytes 4718600 | tf_op jit(solution)/shard_map/ppermute | solution.py:290
  405.5 38.0 %collective-permute-start.44 = (bf16[128,6144]{1,0:T(8,128)(2,1)S(1)}, bf16[128,6144]{1,0:T(8,128)(2,1)S(1)}, u32[]{:S(2)}, u32[]{:S(2)}) collective-permute-start(bf16[128,6144]{1,0:T(8,128)(2,1)S(1)} %add_convert_fusion.2), channel_id=1, source_target_pairs={{0,8},{2,10},{4,12},{6,14},{24,16},{26,18},{28,20},{30,22},{1,9},{... | collective-permute-start | bytes 4718600 | tf_op jit(solution)/shard_map/ppermute | solution.py:290
  411.6 37.4 %collective-permute-start.41 = (bf16[128,6144]{1,0:T(8,128)(2,1)S(1)}, bf16[128,6144]{1,0:T(8,128)(2,1)S(1)}, u32[]{:S(2)}, u32[]{:S(2)}) collective-permute-start(bf16[128,6144]{1,0:T(8,128)(2,1)S(1)} %copy-done.14), channel_id=1, source_target_pairs={{0,2},{2,0},{4,6},{6,4},{8,10},{10,8},{12,14},{14,12},{16,18},{18,... | collective-permute-start | bytes 4718600 | tf_op jit(solution)/shard_map/ppermute | solution.py:252
  416.8 62.7 %collective-permute-start.37 = (bf16[128,6144]{1,0:T(8,128)(2,1)S(1)}, bf16[128,6144]{1,0:T(8,128)(2,1)S(1)}, u32[]{:S(2)}, u32[]{:S(2)}) collective-permute-start(bf16[128,6144]{1,0:T(8,128)(2,1)S(1)} %copy-done.12), channel_id=1, source_target_pairs={{0,2},{2,0},{4,6},{6,4},{8,10},{10,8},{12,14},{14,12},{16,18},{18,... | collective-permute-start | bytes 4718600 | tf_op jit(solution)/shard_map/ppermute | solution.py:252
  (60 other events, 1087.6 us)

commit v4 on v3

--- a/solution.py
+++ b/solution.py
@@ -50,10 +50,14 @@
 
 
 def up_kernel(per_owner, meta, *refs):
-    parts, refs = refs[:PLANE + 1], refs[PLANE + 1:]
+    count_of = len(refs) - 11
+    parts, refs = refs[:count_of], refs[count_of:]
     w_ref, own_ref, send_ref, rows, held, own, send, row_sems, sems, own_sems, send_sems = refs
     count = meta[0]
-    places = [rows.at[0], rows.at[1], rows.at[2], rows.at[3, pl.ds(0, HALF)], rows.at[3, pl.ds(HALF, HALF)]]
+    places, first = [], 0
+    for part in parts:
+        places.append(rows.at[first // BLK, pl.ds(first % BLK, part.shape[0])])
+        first += part.shape[0]
     copies = [pltpu.make_async_copy(*ends, row_sems.at[at]) for at, ends in enumerate(zip(parts, places))]
     for copy in copies:
         copy.start()
@@ -234,7 +238,7 @@
 
 def add_diagonal(over_x, over_y, x_add, y_add):
     feat = over_x.shape[1]
-    steps = 6 if feat % (6 * BLK) == 0 else 1
+    steps = 3
     upper = pl.BlockSpec((HALF, feat // steps), lambda i: (0, i))
     lower = pl.BlockSpec((HALF, feat // steps), lambda i: (1, i))
     return pl.pallas_call(
@@ -336,11 +340,13 @@
     up0 = up(0, tokens, side0, diag0)
     outward, side2, diag1, up0 = together(outward, side2, diag1, up0)
     last = jnp.where(inner, across, outward)
-    diag2, side3 = corner(*side2), sides(last)
-    part0, up1 = down(0, up0), up(1, near, side1, diag1)
-    side3, diag2, part0, up1 = together(side3, diag2, part0, up1)
-    diag3, cross0 = corner(*side3), cross(part0)
-    part1, up2 = down(1, up1), up(2, far, side2, diag2)
+    diag2 = corner(*side2)
+    side3 = [swap(last[rows], bit) for bit in (1, 2) for rows in (slice(0, HALF), slice(HALF, BLK))]
+    part0, up1, up2 = down(0, up0), up(1, near, side1, diag1), up(2, far, side2, diag2)
+    side3, part0, up1, up2 = together(side3, part0, up1, up2)
+    diag3, cross0 = (swap(side3[0], 2), swap(side3[3], 1)), cross(part0)
+    part1 = down(1, up1)
+    diag3, part1 = together(diag3, part1)
     up3 = up(3, last, side3, diag3)
     cross0, part1, up2, up3 = together(cross0, part1, up2, up3)
     cross1, part2, part3 = cross(part1), down(2, up2), down(3, up3)

time: 487 us -> 484 us (level)
    ppermute x34 -> x36, starting transfers between devices: 37.5 us -> 43 us  [swap(): lax.ppermute(value, 'wa', [(w, w ^ bits) for w in range(LAYERS * PLANE)])]
    ppermute x34 -> x36, waiting for transfers between devices: 240 us -> 236 us  [swap(): lax.ppermute(value, 'wa', [(w, w ^ bits) for w in range(LAYERS * PLANE)])]
    unnamed x76 -> x84, local copies, waits for them, and re-layouts: 13.7 us -> 13.1 us
  transfers between devices with their start and end apart: 46 -> 48, of which waited for: 22 -> 26; matrix products, arithmetic and copies ran while one was open for 4% -> 4% of each run, Pallas kernels for 25% -> 25%
where the time goes in v4:
time: 484 us; the launch traced here: 483 us
  waiting for transfers between devices  264 us (55%)
  Pallas kernels  118 us (24%)
  starting transfers between devices  62.4 us (13%)
  local copies, waits for them, and re-layouts  19.9 us (4%)
  other arithmetic  17.3 us (4%)
    ppermute x36, waiting for transfers between devices, swap(): lax.ppermute(value, 'wa', [(w, w ^ bits) for w in range(LAYERS * PLANE)])  236 us
    pallas_call x4, Pallas kernels, down_group(): pl.pallas_call(functools.partial(down_kernel, per_owner, own.shape[0]), i...  57.6 us
    pallas_call x4, Pallas kernels, up_group(): pl.pallas_call(functools.partial(up_kernel, per_owner), in_specs=[pl.Bloc...  45.4 us
    ppermute x36, starting transfers between devices, swap(): lax.ppermute(value, 'wa', [(w, w ^ bits) for w in range(LAYERS * PLANE)])  43 us
    ppermute x8, waiting for transfers between devices, along_z(): return lax.ppermute(value, 'wa', pairs)  25.6 us
    ppermute x8, starting transfers between devices, along_z(): return lax.ppermute(value, 'wa', pairs)  18.8 us
    pallas_call x4, Pallas kernels, add_diagonal(): pl.pallas_call(add_kernel, grid=(steps,), in_specs=[upper, lower, upper,...  15.3 us
    unnamed x84, local copies, waits for them, and re-layouts  13.1 us
  transfers between devices with their start and end apart: 48, of which 26 were waited for; matrix products, arithmetic and copies ran while one was open for 4% of the time, Pallas kernels for 25%

profile of v4, /device:TPU:0, one launch (start us, length us, event | category | flops | bytes accessed | tf_op | source)
XLA Modules:
  0.0 482.9 jit_solution(372444792502150448)
XLA Ops:
  7.9 29.9 %collective-permute-done.refs_0_ = bf16[128,6144]{1,0:T(8,128)(2,1)} collective-permute-done((bf16[128,6144]{1,0:T(8,128)(2,1)}, bf16[128,6144]{1,0:T(8,128)(2,1)}, u32[]{:S(2)}, u32[]{:S(2)}) %collective-permute-start) | collective-permute-done | bytes 1572896 | tf_op jit(solution)/shard_map/ppermute | solution.py:256
  50.3 13.7 %collective-permute-done.8.refs_3_ = bf16[64,6144]{1,0:T(8,128)(2,1)} collective-permute-done((bf16[64,6144]{1,0:T(8,128)(2,1)}, bf16[64,6144]{1,0:T(8,128)(2,1)}, u32[]{:S(2)}, u32[]{:S(2)}) %collective-permute-start.8) | collective-permute-done | bytes 786464 | tf_op jit(solution)/shard_map/ppermute | solution.py:256
  65.5 32.5 %collective-permute-done.9.refs_4_ = bf16[64,6144]{1,0:T(8,128)(2,1)S(1)} collective-permute-done((bf16[64,6144]{1,0:T(8,128)(2,1)S(1)}, bf16[64,6144]{1,0:T(8,128)(2,1)S(1)}, u32[]{:S(2)}, u32[]{:S(2)}) %collective-permute-start.9) | collective-permute-done | bytes 786464 | tf_op jit(solution)/shard_map/ppermute | solution.py:256
  111.3 11.2 %up_group.4 = (f32[52,128,128]{2,1,0:T(8,128)}, bf16[52,128,128]{2,1,0:T(8,128)(2,1)}) custom-call(s32[59]{0:T(128)} %get-tuple-element.246.meta, bf16[128,6144]{1,0:T(8,128)(2,1)} %refs_0_.1, bf16[128,6144]{1,0:T(8,128)(2,1)} %copy-done.5, bf16[128,6144]{1,0:T(8,128)(2,1)} %collective-permute-done.3.refs_2_, ...), custom_call_target="tpu_custom_call" | custom-call | flops 201326592 | bytes 1572864 | tf_op jit(solution)/shard_map/up_group/pallas_call | solution.py:116
  122.5 29.8 %collective-permute-done.13.refs_3_ = bf16[64,6144]{1,0:T(8,128)(2,1)S(1)} collective-permute-done((bf16[64,6144]{1,0:T(8,128)(2,1)}, bf16[64,6144]{1,0:T(8,128)(2,1)S(1)}, u32[]{:S(2)}, u32[]{:S(2)}) %collective-permute-start.13) | collective-permute-done | bytes 786464 | tf_op jit(solution)/shard_map/ppermute | solution.py:256
  162.0 12.4 %collective-permute-done.20.refs_3_ = bf16[64,6144]{1,0:T(8,128)(2,1)S(1)} collective-permute-done((bf16[64,6144]{1,0:T(8,128)(2,1)S(1)}, bf16[64,6144]{1,0:T(8,128)(2,1)S(1)}, u32[]{:S(2)}, u32[]{:S(2)}) %collective-permute-start.20) | collective-permute-done | bytes 786464 | tf_op jit(solution)/shard_map/ppermute | solution.py:256
  177.7 11.1 %up_group.5 = (f32[52,128,128]{2,1,0:T(8,128)}, bf16[52,128,128]{2,1,0:T(8,128)(2,1)}) custom-call(s32[59]{0:T(128)} %get-tuple-element.245.meta, bf16[128,6144]{1,0:T(8,128)(2,1)} %collective-permute-done.refs_0_, bf16[128,6144]{1,0:T(8,128)(2,1)} %copy-done.2, bf16[128,6144]{1,0:T(8,128)(2,1)} %copy-done.3, bf16[64,6144]{1,0:T(8,128)(2,1)} %copy-done.27, ...), custom_call_target="tpu_custom_call" | custom-call | flops 201326592 | bytes 1572864 | tf_op jit(solution)/shard_map/up_group/pallas_call | solution.py:116
  188.8 11.1 %up_group.6 = (f32[52,128,128]{2,1,0:T(8,128)}, bf16[52,128,128]{2,1,0:T(8,128)(2,1)}) custom-call(s32[59]{0:T(128)} %get-tuple-element.244.meta, bf16[128,6144]{1,0:T(8,128)(2,1)} %copy-done.1, bf16[128,6144]{1,0:T(8,128)(2,1)} %collective-permute-done.11.refs_1_, bf16[128,6144]{1,0:T(8,128)(2,1)} %collective-permute-done.12.refs_2_, ...), custom_call_target="tpu_custom_call" | custom-call | flops 201326592 | bytes 1572864 | tf_op jit(solution)/shard_map/up_group/pallas_call | solution.py:116
  201.1 14.7 %down_group.4 = (bf16[128,6144]{1,0:T(8,128)(2,1)}, bf16[128,6144]{1,0:T(8,128)(2,1)}, bf16[128,6144]{1,0:T(8,128)(2,1)}, bf16[64,6144]{1,0:T(8,128)(2,1)}, bf16[64,6144]{1,0:T(8,128)(2,1)}) custom-call(s32[59]{0:T(128)} %get-tuple-element.246.meta, f32[52,128,128]{2,1,0:T(8,128)} %get-tuple-element.135.own_ref, bf16[52,128,128]{2,1,0:T(8,128)(2,1)} %copy-done.6, ...), custom_call_target="tpu_custom_call" | custom-call | flops 201326592 | bytes 1572864 | tf_op jit(solution)/shard_map/down_group/pallas_call | solution.py:214
  221.4 14.6 %down_group.5 = (bf16[128,6144]{1,0:T(8,128)(2,1)}, bf16[128,6144]{1,0:T(8,128)(2,1)}, bf16[128,6144]{1,0:T(8,128)(2,1)}, bf16[64,6144]{1,0:T(8,128)(2,1)}, bf16[64,6144]{1,0:T(8,128)(2,1)}) custom-call(s32[59]{0:T(128)} %get-tuple-element.245.meta, f32[52,128,128]{2,1,0:T(8,128)} %get-tuple-element.154.own_ref, bf16[52,128,128]{2,1,0:T(8,128)(2,1)} %copy-done.8, ...), custom_call_target="tpu_custom_call" | custom-call | flops 201326592 | bytes 1572864 | tf_op jit(solution)/shard_map/down_group/pallas_call | solution.py:214
  237.8 12.0 %up_group.7 = (f32[52,128,128]{2,1,0:T(8,128)}, bf16[52,128,128]{2,1,0:T(8,128)(2,1)}) custom-call(s32[59]{0:T(128)} %get-tuple-element.243.meta, bf16[128,6144]{1,0:T(8,128)(2,1)} %copy-done, bf16[64,6144]{1,0:T(8,128)(2,1)} %copy-done.25, bf16[64,6144]{1,0:T(8,128)(2,1)} %copy-done.29, bf16[64,6144]{1,0:T(8,128)(2,1)} %copy-done.26, ...), custom_call_target="tpu_custom_call" | custom-call | flops 201326592 | bytes 1572864 | tf_op jit(solution)/shard_map/up_group/pallas_call | solution.py:116
  261.4 14.4 %down_group.7 = (bf16[128,6144]{1,0:T(8,128)(2,1)}, bf16[128,6144]{1,0:T(8,128)(2,1)}, bf16[128,6144]{1,0:T(8,128)(2,1)}, bf16[64,6144]{1,0:T(8,128)(2,1)}, bf16[64,6144]{1,0:T(8,128)(2,1)}) custom-call(s32[59]{0:T(128)} %get-tuple-element.243.meta, f32[52,128,128]{2,1,0:T(8,128)} %get-tuple-element.183.own_ref, bf16[52,128,128]{2,1,0:T(8,128)(2,1)} %copy-done.9, ...), custom_call_target="tpu_custom_call" | custom-call | flops 201326592 | bytes 1572864 | tf_op jit(solution)/shard_map/down_group/pallas_call | solution.py:214
  277.1 13.9 %down_group.6 = (bf16[128,6144]{1,0:T(8,128)(2,1)}, bf16[128,6144]{1,0:T(8,128)(2,1)}, bf16[128,6144]{1,0:T(8,128)(2,1)}, bf16[64,6144]{1,0:T(8,128)(2,1)}, bf16[64,6144]{1,0:T(8,128)(2,1)}) custom-call(s32[59]{0:T(128)} %get-tuple-element.244.meta, f32[52,128,128]{2,1,0:T(8,128)} %get-tuple-element.176.own_ref, bf16[52,128,128]{2,1,0:T(8,128)(2,1)} %copy-done.7, ...), custom_call_target="tpu_custom_call" | custom-call | flops 201326592 | bytes 1572864 | tf_op jit(solution)/shard_map/down_group/pallas_call | solution.py:214
  295.3 16.4 %collective-permute-done.31.x_add = bf16[64,6144]{1,0:T(8,128)(2,1)S(1)} collective-permute-done((bf16[64,6144]{1,0:T(8,128)(2,1)}, bf16[64,6144]{1,0:T(8,128)(2,1)S(1)}, u32[]{:S(2)}, u32[]{:S(2)}) %collective-permute-start.31) | collective-permute-done | bytes 786464 | tf_op jit(solution)/shard_map/ppermute | solution.py:256
  318.0 9.8 %collective-permute-done.33.x_add = bf16[64,6144]{1,0:T(8,128)(2,1)S(1)} collective-permute-done((bf16[64,6144]{1,0:T(8,128)(2,1)}, bf16[64,6144]{1,0:T(8,128)(2,1)S(1)}, u32[]{:S(2)}, u32[]{:S(2)}) %collective-permute-start.33) | collective-permute-done | bytes 786464 | tf_op jit(solution)/shard_map/ppermute | solution.py:256
  337.8 29.7 %collective-permute-done.37 = bf16[128,6144]{1,0:T(8,128)(2,1)S(1)} collective-permute-done((bf16[128,6144]{1,0:T(8,128)(2,1)}, bf16[128,6144]{1,0:T(8,128)(2,1)S(1)}, u32[]{:S(2)}, u32[]{:S(2)}) %collective-permute-start.37) | collective-permute-done | bytes 1572896 | tf_op jit(solution)/shard_map/ppermute | solution.py:256
  371.9 5.8 %collective-permute-start.41 = (bf16[128,6144]{1,0:T(8,128)(2,1)S(1)}, bf16[128,6144]{1,0:T(8,128)(2,1)}, u32[]{:S(2)}, u32[]{:S(2)}) collective-permute-start(bf16[128,6144]{1,0:T(8,128)(2,1)S(1)} %add_convert_fusion.5), channel_id=1, source_target_pairs={{0,8},{2,10},{4,12},{6,14},{24,16},{26,18},{28,20},{30,22},{1,9},{... | collective-permute-start | bytes 4718600 | tf_op jit(solution)/shard_map/ppermute | solution.py:294
  381.5 3.9 add_diagonal.6
  385.4 13.9 %collective-permute-done.35 = bf16[128,6144]{1,0:T(8,128)(2,1)} collective-permute-done((bf16[128,6144]{1,0:T(8,128)(2,1)}, bf16[128,6144]{1,0:T(8,128)(2,1)}, u32[]{:S(2)}, u32[]{:S(2)}) %collective-permute-start.35) | collective-permute-done | bytes 1572896 | tf_op jit(solution)/shard_map/ppermute | solution.py:256
  403.5 5.0 %collective-permute-start.46 = (bf16[128,6144]{1,0:T(8,128)(2,1)S(1)}, bf16[128,6144]{1,0:T(8,128)(2,1)S(1)}, u32[]{:S(2)}, u32[]{:S(2)}) collective-permute-start(bf16[128,6144]{1,0:T(8,128)(2,1)S(1)} %add_convert_fusion.2), channel_id=1, source_target_pairs={{0,8},{2,10},{4,12},{6,14},{24,16},{26,18},{28,20},{30,22},{1,9},{... | collective-permute-start | bytes 4718600 | tf_op jit(solution)/shard_map/ppermute | solution.py:294
  414.4 25.5 %collective-permute-done.46 = bf16[128,6144]{1,0:T(8,128)(2,1)S(1)} collective-permute-done((bf16[128,6144]{1,0:T(8,128)(2,1)S(1)}, bf16[128,6144]{1,0:T(8,128)(2,1)S(1)}, u32[]{:S(2)}, u32[]{:S(2)}) %collective-permute-start.46) | collective-permute-done | bytes 1572896 | tf_op jit(solution)/shard_map/ppermute | solution.py:294
  441.8 4.1 collective-permute-done.43
  450.3 25.8 %collective-permute-done.39 = bf16[128,6144]{1,0:T(8,128)(2,1)S(1)} collective-permute-done((bf16[128,6144]{1,0:T(8,128)(2,1)S(1)}, bf16[128,6144]{1,0:T(8,128)(2,1)S(1)}, u32[]{:S(2)}, u32[]{:S(2)}) %collective-permute-start.39) | collective-permute-done | bytes 1572896 | tf_op jit(solution)/shard_map/ppermute | solution.py:256
  476.4 4.0 collective-permute-done.45
  (210 shorter events, 117.0 us)
Async XLA Ops:
  0.0 37.7 %collective-permute-start = (bf16[128,6144]{1,0:T(8,128)(2,1)}, bf16[128,6144]{1,0:T(8,128)(2,1)}, u32[]{:S(2)}, u32[]{:S(2)}) collective-permute-start(bf16[128,6144]{1,0:T(8,128)(2,1)} %refs_0_.1), channel_id=1, source_target_pairs={{0,8},{2,10},{4,12},{6,14},{8,0},{10,2},{12,4},{14,6},{16,24},{18,... | collective-permute-start | bytes 4718600 | tf_op jit(solution)/shard_map/ppermute | solution.py:256
  44.7 53.2 %collective-permute-start.4 = (bf16[128,6144]{1,0:T(8,128)(2,1)}, bf16[128,6144]{1,0:T(8,128)(2,1)}, u32[]{:S(2)}, u32[]{:S(2)}) collective-permute-start(bf16[128,6144]{1,0:T(8,128)(2,1)} %collective-permute-done.refs_0_), channel_id=1, source_target_pairs={{8,16},{10,18},{12,20},{14,22},{16,8},{18,10},{20,12},{22,14},{9,1... | collective-permute-start | bytes 4718600 | tf_op jit(solution)/shard_map/ppermute | solution.py:294
  46.5 51.4 %collective-permute-start.6 = (bf16[128,6144]{1,0:T(8,128)(2,1)}, bf16[128,6144]{1,0:T(8,128)(2,1)S(1)}, u32[]{:S(2)}, u32[]{:S(2)}) collective-permute-start(bf16[128,6144]{1,0:T(8,128)(2,1)} %collective-permute-done.refs_0_), channel_id=1, source_target_pairs={{0,2},{2,0},{4,6},{6,4},{8,10},{10,8},{12,14},{14,12},{16,18},{18,... | collective-permute-start | bytes 4718600 | tf_op jit(solution)/shard_map/ppermute | solution.py:256
  47.1 50.8 %collective-permute-start.7 = (bf16[128,6144]{1,0:T(8,128)(2,1)}, bf16[128,6144]{1,0:T(8,128)(2,1)S(1)}, u32[]{:S(2)}, u32[]{:S(2)}) collective-permute-start(bf16[128,6144]{1,0:T(8,128)(2,1)} %collective-permute-done.refs_0_), channel_id=1, source_target_pairs={{0,4},{2,6},{4,0},{6,2},{8,12},{10,14},{12,8},{14,10},{16,20},{18,... | collective-permute-start | bytes 4718600 | tf_op jit(solution)/shard_map/ppermute | solution.py:256
  47.6 52.4 %collective-permute-start.5 = (bf16[128,6144]{1,0:T(8,128)(2,1)}, bf16[128,6144]{1,0:T(8,128)(2,1)}, u32[]{:S(2)}, u32[]{:S(2)}) collective-permute-start(bf16[128,6144]{1,0:T(8,128)(2,1)} %collective-permute-done.1), channel_id=1, source_target_pairs={{8,0},{10,2},{12,4},{14,6},{16,24},{18,26},{20,28},{22,30},{9,1},{... | collective-permute-start | bytes 4718600 | tf_op jit(solution)/shard_map/ppermute | solution.py:294
  101.6 50.8 %collective-permute-start.11 = (bf16[128,6144]{1,0:T(8,128)(2,1)S(1)}, bf16[128,6144]{1,0:T(8,128)(2,1)}, u32[]{:S(2)}, u32[]{:S(2)}) collective-permute-start(bf16[128,6144]{1,0:T(8,128)(2,1)S(1)} %broadcast_select_fusion.1.refs_0_), channel_id=1, source_target_pairs={{0,2},{2,0},{4,6},{6,4},{8,10},{10,8},{12,14},{14,12},{16,18},{18,... | collective-permute-start | bytes 4718600 | tf_op jit(solution)/shard_map/ppermute | solution.py:256
  102.3 50.1 %collective-permute-start.12 = (bf16[128,6144]{1,0:T(8,128)(2,1)S(1)}, bf16[128,6144]{1,0:T(8,128)(2,1)}, u32[]{:S(2)}, u32[]{:S(2)}) collective-permute-start(bf16[128,6144]{1,0:T(8,128)(2,1)S(1)} %broadcast_select_fusion.1.refs_0_), channel_id=1, source_target_pairs={{0,4},{2,6},{4,0},{6,2},{8,12},{10,14},{12,8},{14,10},{16,20},{18,... | collective-permute-start | bytes 4718600 | tf_op jit(solution)/shard_map/ppermute | solution.py:256
  102.8 49.6 %collective-permute-start.10 = (bf16[128,6144]{1,0:T(8,128)(2,1)}, bf16[128,6144]{1,0:T(8,128)(2,1)}, u32[]{:S(2)}, u32[]{:S(2)}) collective-permute-start(bf16[128,6144]{1,0:T(8,128)(2,1)} %collective-permute-done.4), channel_id=1, source_target_pairs={{8,0},{10,2},{12,4},{14,6},{16,24},{18,26},{20,28},{22,30},{9,1},{... | collective-permute-start | bytes 4718600 | tf_op jit(solution)/shard_map/ppermute | solution.py:294
  106.3 46.0 %collective-permute-start.13 = (bf16[64,6144]{1,0:T(8,128)(2,1)}, bf16[64,6144]{1,0:T(8,128)(2,1)S(1)}, u32[]{:S(2)}, u32[]{:S(2)}) collective-permute-start(bf16[64,6144]{1,0:T(8,128)(2,1)} %slice.44), channel_id=1, source_target_pairs={{0,4},{2,6},{4,0},{6,2},{8,12},{10,14},{12,8},{14,10},{16,20},{18,... | collective-permute-start | bytes 2359304 | tf_op jit(solution)/shard_map/ppermute | solution.py:256
  107.9 44.4 %collective-permute-start.14 = (bf16[64,6144]{1,0:T(8,128)(2,1)S(1)}, bf16[64,6144]{1,0:T(8,128)(2,1)}, u32[]{:S(2)}, u32[]{:S(2)}) collective-permute-start(bf16[64,6144]{1,0:T(8,128)(2,1)S(1)} %slice.45), channel_id=1, source_target_pairs={{0,2},{2,0},{4,6},{6,4},{8,10},{10,8},{12,14},{14,12},{16,18},{18,... | collective-permute-start | bytes 2359304 | tf_op jit(solution)/shard_map/ppermute | solution.py:256
  157.0 42.9 %collective-permute-start.19 = (bf16[52,128,128]{2,1,0:T(8,128)(2,1)}, bf16[52,128,128]{2,1,0:T(8,128)(2,1)S(1)}, u32[]{:S(2)}, u32[]{:S(2)}) collective-permute-start(bf16[52,128,128]{2,1,0:T(8,128)(2,1)} %get-tuple-element.136), channel_id=1, source_target_pairs={{0,1},{1,0},{2,3},{3,2},{4,5},{5,4},{6,7},{7,6},{8,9},{9,8},{10,11... | collective-permute-start | bytes 5111816 | tf_op jit(solution)/shard_map/ppermute | solution.py:324
  159.8 56.0 %collective-permute-start.15 = (bf16[64,6144]{1,0:T(8,128)(2,1)S(1)}, bf16[64,6144]{1,0:T(8,128)(2,1)S(1)}, u32[]{:S(2)}, u32[]{:S(2)}) collective-permute-start(bf16[64,6144]{1,0:T(8,128)(2,1)S(1)} %get-tuple-element.242), channel_id=1, source_target_pairs={{0,2},{2,0},{4,6},{6,4},{8,10},{10,8},{12,14},{14,12},{16,18},{18,... | collective-permute-start | bytes 2359304 | tf_op jit(solution)/shard_map/ppermute | solution.py:256
  160.5 55.4 %collective-permute-start.17 = (bf16[64,6144]{1,0:T(8,128)(2,1)S(1)}, bf16[64,6144]{1,0:T(8,128)(2,1)S(1)}, u32[]{:S(2)}, u32[]{:S(2)}) collective-permute-start(bf16[64,6144]{1,0:T(8,128)(2,1)S(1)} %get-tuple-element.242), channel_id=1, source_target_pairs={{0,4},{2,6},{4,0},{6,2},{8,12},{10,14},{12,8},{14,10},{16,20},{18,... | collective-permute-start | bytes 2359304 | tf_op jit(solution)/shard_map/ppermute | solution.py:256
  174.4 41.4 %collective-permute-start.16 = (bf16[64,6144]{1,0:T(8,128)(2,1)S(1)}, bf16[64,6144]{1,0:T(8,128)(2,1)S(1)}, u32[]{:S(2)}, u32[]{:S(2)}) collective-permute-start(bf16[64,6144]{1,0:T(8,128)(2,1)S(1)} %get-tuple-element.241), channel_id=1, source_target_pairs={{0,2},{2,0},{4,6},{6,4},{8,10},{10,8},{12,14},{14,12},{16,18},{18,... | collective-permute-start | bytes 2359304 | tf_op jit(solution)/shard_map/ppermute | solution.py:256
  176.2 39.7 %collective-permute-start.18 = (bf16[64,6144]{1,0:T(8,128)(2,1)S(1)}, bf16[64,6144]{1,0:T(8,128)(2,1)S(1)}, u32[]{:S(2)}, u32[]{:S(2)}) collective-permute-start(bf16[64,6144]{1,0:T(8,128)(2,1)S(1)} %get-tuple-element.241), channel_id=1, source_target_pairs={{0,4},{2,6},{4,0},{6,2},{8,12},{10,14},{12,8},{14,10},{16,20},{18,... | collective-permute-start | bytes 2359304 | tf_op jit(solution)/shard_map/ppermute | solution.py:256
  254.4 36.6 %collective-permute-start.27 = (bf16[64,6144]{1,0:T(8,128)(2,1)S(1)}, bf16[64,6144]{1,0:T(8,128)(2,1)}, u32[]{:S(2)}, u32[]{:S(2)}) collective-permute-start(bf16[64,6144]{1,0:T(8,128)(2,1)S(1)} %copy-done.40), channel_id=1, source_target_pairs={{0,4},{2,6},{4,0},{6,2},{8,12},{10,14},{12,8},{14,10},{16,20},{18,... | collective-permute-start | bytes 2359304 | tf_op jit(solution)/shard_map/ppermute | solution.py:256
  330.0 37.5 %collective-permute-start.37 = (bf16[128,6144]{1,0:T(8,128)(2,1)}, bf16[128,6144]{1,0:T(8,128)(2,1)S(1)}, u32[]{:S(2)}, u32[]{:S(2)}) collective-permute-start(bf16[128,6144]{1,0:T(8,128)(2,1)} %get-tuple-element.216), channel_id=1, source_target_pairs={{0,2},{2,0},{4,6},{6,4},{8,10},{10,8},{12,14},{14,12},{16,18},{18,... | collective-permute-start | bytes 4718600 | tf_op jit(solution)/shard_map/ppermute | solution.py:256
  331.7 37.6 %collective-permute-start.38 = (bf16[128,6144]{1,0:T(8,128)(2,1)}, bf16[128,6144]{1,0:T(8,128)(2,1)}, u32[]{:S(2)}, u32[]{:S(2)}) collective-permute-start(bf16[128,6144]{1,0:T(8,128)(2,1)} %get-tuple-element.217), channel_id=1, source_target_pairs={{0,4},{2,6},{4,0},{6,2},{8,12},{10,14},{12,8},{14,10},{16,20},{18,... | collective-permute-start | bytes 4718600 | tf_op jit(solution)/shard_map/ppermute | solution.py:256
  336.2 63.0 %collective-permute-start.35 = (bf16[128,6144]{1,0:T(8,128)(2,1)}, bf16[128,6144]{1,0:T(8,128)(2,1)}, u32[]{:S(2)}, u32[]{:S(2)}) collective-permute-start(bf16[128,6144]{1,0:T(8,128)(2,1)} %get-tuple-element.213), channel_id=1, source_target_pairs={{0,2},{2,0},{4,6},{6,4},{8,10},{10,8},{12,14},{14,12},{16,18},{18,... | collective-permute-start | bytes 4718600 | tf_op jit(solution)/shard_map/ppermute | solution.py:256
  336.5 64.2 %collective-permute-start.36 = (bf16[128,6144]{1,0:T(8,128)(2,1)}, bf16[128,6144]{1,0:T(8,128)(2,1)}, u32[]{:S(2)}, u32[]{:S(2)}) collective-permute-start(bf16[128,6144]{1,0:T(8,128)(2,1)} %get-tuple-element.214), channel_id=1, source_target_pairs={{0,4},{2,6},{4,0},{6,2},{8,12},{10,14},{12,8},{14,10},{16,20},{18,... | collective-permute-start | bytes 4718600 | tf_op jit(solution)/shard_map/ppermute | solution.py:256
  371.9 38.3 %collective-permute-start.41 = (bf16[128,6144]{1,0:T(8,128)(2,1)S(1)}, bf16[128,6144]{1,0:T(8,128)(2,1)}, u32[]{:S(2)}, u32[]{:S(2)}) collective-permute-start(bf16[128,6144]{1,0:T(8,128)(2,1)S(1)} %add_convert_fusion.5), channel_id=1, source_target_pairs={{0,8},{2,10},{4,12},{6,14},{24,16},{26,18},{28,20},{30,22},{1,9},{... | collective-permute-start | bytes 4718600 | tf_op jit(solution)/shard_map/ppermute | solution.py:294
  408.5 37.4 %collective-permute-start.43 = (bf16[128,6144]{1,0:T(8,128)(2,1)S(1)}, bf16[128,6144]{1,0:T(8,128)(2,1)S(1)}, u32[]{:S(2)}, u32[]{:S(2)}) collective-permute-start(bf16[128,6144]{1,0:T(8,128)(2,1)S(1)} %copy-done.12), channel_id=1, source_target_pairs={{0,2},{2,0},{4,6},{6,4},{8,10},{10,8},{12,14},{14,12},{16,18},{18,... | collective-permute-start | bytes 4718600 | tf_op jit(solution)/shard_map/ppermute | solution.py:256
  409.1 37.8 %collective-permute-start.44 = (bf16[128,6144]{1,0:T(8,128)(2,1)S(1)}, bf16[128,6144]{1,0:T(8,128)(2,1)S(1)}, u32[]{:S(2)}, u32[]{:S(2)}) collective-permute-start(bf16[128,6144]{1,0:T(8,128)(2,1)S(1)} %copy-done.13), channel_id=1, source_target_pairs={{0,4},{2,6},{4,0},{6,2},{8,12},{10,14},{12,8},{14,10},{16,20},{18,... | collective-permute-start | bytes 4718600 | tf_op jit(solution)/shard_map/ppermute | solution.py:256
  412.9 63.2 %collective-permute-start.39 = (bf16[128,6144]{1,0:T(8,128)(2,1)S(1)}, bf16[128,6144]{1,0:T(8,128)(2,1)S(1)}, u32[]{:S(2)}, u32[]{:S(2)}) collective-permute-start(bf16[128,6144]{1,0:T(8,128)(2,1)S(1)} %copy-done.10), channel_id=1, source_target_pairs={{0,2},{2,0},{4,6},{6,4},{8,10},{10,8},{12,14},{14,12},{16,18},{18,... | collective-permute-start | bytes 4718600 | tf_op jit(solution)/shard_map/ppermute | solution.py:256
  (66 other events, 1222.8 us)
